TPU v7x, 32 devices: a whole 2x2x4 slice. The times are simulated.
32 devices in a mesh: ctx: 16 (over z, y, x), head: 2 (over core).
Axes of the slice: x: 2, y: 2, z: 4, core: 2. Of those that a mesh axis runs over, the one named last changes fastest.
Arguments:
- queries: bfloat16 [4096, 4096], P('ctx', 'head'), may hold values from -15 to 15
- key_rows: bfloat16 [4096, 4096], P('ctx', 'head'), may hold values from -4 to 4
- value_rows: bfloat16 [4096, 4096], P('ctx', 'head'), may hold values from -32 to 32
- cotangent: bfloat16 [4096, 4096], P('ctx', 'head'), may hold values from -6 to 6
- norm_gain: float32 [4096], P('head'), may hold values from 0.1 to 1.9
- pairing: int32 [16], replicated, may hold values from 0 to 15, as said below
Outputs:
- mixed: bfloat16 [4096, 4096], P('ctx', 'head')
- grad_query: bfloat16 [4096, 4096], P('ctx', 'head')
- grad_key: bfloat16 [4096, 4096], P('ctx', 'head')
- grad_value: bfloat16 [4096, 4096], P('ctx', 'head')
Inputs may be any that keep to these rules, and one draw needn't show every extreme that they name: pairing is a permutation of the 16 blocks, and pairing[b] differs from b.
All inputs are finite; a program needn't handle non-finite values.
Results may differ from a plain program's by a relative error of at most 0.012.
Values may be sent and summed in bfloat16 or wider, within the bound.
No kernel may reach another device: no remote copies, remote signals or barrier semaphores. Data moves between devices by JAX's collectives and lax.ppermute only.
A program may use at most 64 MiB of HBM per device.

v0:
```python
import math

import jax
import jax.numpy as jnp
from jax import lax
from jax.sharding import PartitionSpec as P

H = 32
HD = 128
BLOCK = 256


EPSILON = 1e-05


def from_behind(value, axis, steps):
    count = lax.axis_size(axis)
    first, last = (max(0, -steps), min(count, count - steps))
    return lax.ppermute(value, axis, [(source, source + steps) for source in range(first, last)])


def spread_rows(blocks_in, devices):
    return blocks_in.reshape(
        blocks_in.shape[0], devices, blocks_in.shape[1] // devices, blocks_in.shape[2]
    )


def choose_pieces(pieces, wanted, devices):
    holders = pieces.shape[0]
    stacked = pieces.reshape(holders * devices, pieces.shape[2], pieces.shape[3])
    wanted_grid = jnp.transpose(wanted.reshape(devices, -1))
    position = wanted_grid % holders * devices + wanted_grid // holders
    return jnp.take(stacked, position, axis=0)


def join_rows(pieces):
    return pieces.reshape(pieces.shape[0], pieces.shape[1] * pieces.shape[2], pieces.shape[3])


def window_scores(query_blocks, keys_window, first_block):
    blocks_here = query_blocks.shape[0]
    length = query_blocks.shape[1]
    factor = 1.0 / math.sqrt(query_blocks.shape[3])
    scores = (
        jnp.einsum("bihd,bjhd->bhij", query_blocks, keys_window, preferred_element_type=jnp.float32)
        * factor
    )
    places = jnp.arange(length)
    causal = places[:, None] >= places[None, :]
    earlier = first_block + jnp.arange(blocks_here) > 0
    earlier_mask = jnp.broadcast_to(earlier[:, None, None], (blocks_here, length, length))
    causal_mask = causal[None]
    partner_mask = jnp.ones((blocks_here, length, length), bool)
    allowed = jnp.concatenate([earlier_mask, causal_mask, partner_mask], axis=2)
    return jnp.where(allowed[:, None], scores, -jnp.inf)


def on_device(queries, key_rows, value_rows, cotangent, norm_gain, pairing):
    devices = lax.axis_size("ctx")
    my_index = lax.axis_index("ctx")
    width = queries.shape[1]
    heads_here = width // HD
    blocks_here = queries.shape[0] // BLOCK
    all_blocks = pairing.shape[0]
    shape_four = (blocks_here, BLOCK, heads_here, HD)
    key_blocks = key_rows.reshape(blocks_here, BLOCK, width)
    value_blocks = value_rows.reshape(blocks_here, BLOCK, width)
    arrived = (
        lax.all_to_all(
            spread_rows(key_blocks, devices), "ctx", split_axis=1, concat_axis=1, tiled=True
        ),
        lax.all_to_all(
            spread_rows(value_blocks, devices), "ctx", split_axis=1, concat_axis=1, tiled=True
        ),
    )
    block_range = jnp.arange(all_blocks, dtype=jnp.int32)
    delivered = (
        lax.all_to_all(
            choose_pieces(arrived[0], pairing, devices),
            "ctx",
            split_axis=1,
            concat_axis=1,
            tiled=True,
        ),
        lax.all_to_all(
            choose_pieces(arrived[1], pairing, devices),
            "ctx",
            split_axis=1,
            concat_axis=1,
            tiled=True,
        ),
    )
    partner_keys = join_rows(delivered[0])
    partner_values = join_rows(delivered[1])
    trailing = from_behind((key_blocks[-1], value_blocks[-1]), "ctx", 1)
    prior_keys = jnp.concatenate([trailing[0][None], key_blocks[:-1]], axis=0)
    prior_values = jnp.concatenate([trailing[1][None], value_blocks[:-1]], axis=0)
    keys_window = jnp.concatenate([prior_keys, key_blocks, partner_keys], axis=1).reshape(
        blocks_here, 3 * BLOCK, heads_here, HD
    )
    values_window = jnp.concatenate([prior_values, value_blocks, partner_values], axis=1).reshape(
        blocks_here, 3 * BLOCK, heads_here, HD
    )
    query_blocks = queries.reshape(shape_four)
    first_block = my_index * blocks_here
    scores = window_scores(query_blocks, keys_window, first_block)
    highest = jnp.max(scores, axis=-1, keepdims=True)
    logsum = highest + jnp.log(jnp.sum(jnp.exp(scores - highest), axis=-1, keepdims=True))
    weights = jnp.exp(scores - logsum)
    weights_low = weights.astype(jnp.bfloat16)
    attn = jnp.einsum(
        "bhij,bjhd->bihd", weights_low, values_window, preferred_element_type=jnp.float32
    ).astype(jnp.bfloat16)
    attn_flat = attn.reshape(blocks_here * BLOCK, width).astype(jnp.float32)
    grad_in = norm_gain * cotangent.astype(jnp.float32)
    squares, products = lax.psum(
        (jnp.sum(attn_flat * attn_flat, axis=1), jnp.sum(grad_in * attn_flat, axis=1)), "head"
    )
    features = float(H * HD)
    rms_scale = lax.rsqrt(squares / features + EPSILON)[:, None]
    mixed = (attn_flat * rms_scale * norm_gain).astype(jnp.bfloat16)
    dattn = (
        rms_scale * grad_in - attn_flat * rms_scale**3 * (products / features)[:, None]
    ).astype(jnp.bfloat16)
    dattn_four = dattn.reshape(shape_four)
    delta = jnp.einsum("bihd,bihd->bih", dattn_four, attn, preferred_element_type=jnp.float32)
    dprob = jnp.einsum(
        "bihd,bjhd->bhij", dattn_four, values_window, preferred_element_type=jnp.float32
    )
    dscore = (weights * (dprob - jnp.transpose(delta, (0, 2, 1))[..., None])).astype(jnp.bfloat16)
    factor = 1.0 / math.sqrt(HD)
    grad_query = (
        jnp.einsum("bhij,bjhd->bihd", dscore, keys_window, preferred_element_type=jnp.float32)
        * factor
    ).astype(jnp.bfloat16)
    key_terms = (
        (
            jnp.einsum("bhij,bihd->bjhd", dscore, query_blocks, preferred_element_type=jnp.float32)
            * factor
        )
        .astype(jnp.bfloat16)
        .reshape(blocks_here, 3 * BLOCK, width)
    )
    value_terms = (
        jnp.einsum("bhij,bihd->bjhd", weights_low, dattn_four, preferred_element_type=jnp.float32)
        .astype(jnp.bfloat16)
        .reshape(blocks_here, 3 * BLOCK, width)
    )
    inverse = jnp.zeros((all_blocks,), jnp.int32).at[pairing].set(block_range)
    returned = (
        lax.all_to_all(
            spread_rows(key_terms[:, 2 * BLOCK :], devices),
            "ctx",
            split_axis=1,
            concat_axis=1,
            tiled=True,
        ),
        lax.all_to_all(
            spread_rows(value_terms[:, 2 * BLOCK :], devices),
            "ctx",
            split_axis=1,
            concat_axis=1,
            tiled=True,
        ),
    )
    homeward = (
        lax.all_to_all(
            choose_pieces(returned[0], inverse, devices),
            "ctx",
            split_axis=1,
            concat_axis=1,
            tiled=True,
        ),
        lax.all_to_all(
            choose_pieces(returned[1], inverse, devices),
            "ctx",
            split_axis=1,
            concat_axis=1,
            tiled=True,
        ),
    )
    partner_key_part = join_rows(homeward[0])
    partner_value_part = join_rows(homeward[1])
    leading = from_behind((key_terms[0, :BLOCK], value_terms[0, :BLOCK]), "ctx", -1)
    next_key_part = jnp.concatenate([key_terms[1:, :BLOCK], leading[0][None]], axis=0)
    next_value_part = jnp.concatenate([value_terms[1:, :BLOCK], leading[1][None]], axis=0)
    own_keys = key_terms[:, BLOCK : 2 * BLOCK].astype(jnp.float32)
    own_values = value_terms[:, BLOCK : 2 * BLOCK].astype(jnp.float32)
    grad_key = (
        own_keys + next_key_part.astype(jnp.float32) + partner_key_part.astype(jnp.float32)
    ).astype(jnp.bfloat16)
    grad_value = (
        own_values + next_value_part.astype(jnp.float32) + partner_value_part.astype(jnp.float32)
    ).astype(jnp.bfloat16)
    rows_here = blocks_here * BLOCK
    return (
        mixed,
        grad_query.reshape(rows_here, width),
        grad_key.reshape(rows_here, width),
        grad_value.reshape(rows_here, width),
    )


def solution(mesh):
    placed = (
        P("ctx", "head"),
        P("ctx", "head"),
        P("ctx", "head"),
        P("ctx", "head"),
        P("head"),
        P(),
    )
    return jax.shard_map(
        on_device,
        mesh=mesh,
        in_specs=placed,
        out_specs=(P("ctx", "head"), P("ctx", "head"), P("ctx", "head"), P("ctx", "head")),
        check_vma=False,
    )
```

profile of v0, /device:TPU:14, one launch (start us, length us, event | category | flops | bytes accessed | tf_op | source)
XLA Modules:
  0.0 372.8 jit_solution(512025100780971603)
XLA Ops:
  0.6 31.4 %all_to_all.40 = bf16[1,16,16,2048]{3,2,0,1:T(8,128)(2,1)S(1)} all-to-all(bf16[1,16,16,2048]{3,2,0,1:T(8,128)(2,1)} %bitcast.171), channel_id=1, replica_groups=mesh['ctx'=16,'head'=2] {'ctx'}, dimensions={1} | all-to-all | bytes 2097152 | tf_op jit(solution)/shard_map/all_to_all | solution.py:69
  32.0 6.0 %all-to-all-start = ((bf16[1,16,16,2048]{3,2,0,1:T(8,128)(2,1)}), bf16[1,16,16,2048]{3,2,0,1:T(8,128)(2,1)S(1)}, u32[]{:S(2)}, u32[]{:S(2)}) async-start(bf16[1,16,16,2048]{3,2,0,1:T(8,128)(2,1)} %bitcast.172), calls=%async_computation | async-start | bytes 2097152 | tf_op jit(solution)/shard_map/all_to_all | solution.py:72
  40.0 21.7 %all-to-all-done = bf16[1,16,16,2048]{3,2,0,1:T(8,128)(2,1)S(1)} async-done(((bf16[1,16,16,2048]{3,2,0,1:T(8,128)(2,1)}), bf16[1,16,16,2048]{3,2,0,1:T(8,128)(2,1)S(1)}, u32[]{:S(2)}, u32[]{:S(2)}) %all-to-all-start) | async-done | bytes 1048608 | tf_op jit(solution)/shard_map/all_to_all | solution.py:72
  62.4 1.6 fusion.10
  63.9 5.8 %all-to-all-start.3 = ((bf16[1,16,16,2048]{3,2,0,1:T(8,128)(2,1)}), bf16[1,16,16,2048]{3,2,0,1:T(8,128)(2,1)S(1)}, u32[]{:S(2)}, u32[]{:S(2)}) async-start(bf16[1,16,16,2048]{3,2,0,1:T(8,128)(2,1)} %get-tuple-element.31), calls=%async_computation.3 | async-start | bytes 2097152 | tf_op jit(solution)/shard_map/all_to_all | solution.py:78
  71.1 3.4 collective-permute-start.1
  74.4 3.4 collective-permute-start
  77.8 2.3 copy.61
  81.6 2.7 copy.68
  84.3 8.5 %all-to-all-done.3 = bf16[1,16,16,2048]{3,2,0,1:T(8,128)(2,1)S(1)} async-done(((bf16[1,16,16,2048]{3,2,0,1:T(8,128)(2,1)}), bf16[1,16,16,2048]{3,2,0,1:T(8,128)(2,1)S(1)}, u32[]{:S(2)}, u32[]{:S(2)}) %all-to-all-start.3) | async-done | bytes 1048608 | tf_op jit(solution)/shard_map/all_to_all | solution.py:78
  92.8 7.4 %all-to-all-start.1 = ((bf16[1,16,16,2048]{3,2,0,1:T(8,128)(2,1)}), bf16[1,16,16,2048]{3,2,0,1:T(8,128)(2,1)S(1)}, u32[]{:S(2)}, u32[]{:S(2)}) async-start(bf16[1,16,16,2048]{3,2,0,1:T(8,128)(2,1)} %get-tuple-element.32), calls=%async_computation.1 | async-start | bytes 2097152 | tf_op jit(solution)/shard_map/all_to_all | solution.py:85
  100.5 19.4 %collective-permute-done.1 = bf16[256,2048]{0,1:T(8,128)(2,1)} collective-permute-done((bf16[256,2048]{0,1:T(8,128)(2,1)}, bf16[256,2048]{0,1:T(8,128)(2,1)}, u32[]{:S(2)}, u32[]{:S(2)}) %collective-permute-start.1) | collective-permute-done | bytes 1048608 | tf_op jit(solution)/shard_map/ppermute | solution.py:19
  119.9 2.3 copy.67
  122.1 24.5 %collective-permute-done = bf16[256,2048]{1,0:T(8,128)(2,1)} collective-permute-done((bf16[256,2048]{1,0:T(8,128)(2,1)}, bf16[256,2048]{1,0:T(8,128)(2,1)}, u32[]{:S(2)}, u32[]{:S(2)}) %collective-permute-start) | collective-permute-done | bytes 1048608 | tf_op jit(solution)/shard_map/ppermute | solution.py:19
  146.7 2.3 copy.60
  149.5 3.7 fusion.1
  153.2 2.5 exponential_reduce_fusion
  155.7 2.0 copy-done
  157.7 7.6 %all-to-all-done.1 = bf16[1,16,16,2048]{3,2,0,1:T(8,128)(2,1)S(1)} async-done(((bf16[1,16,16,2048]{3,2,0,1:T(8,128)(2,1)}), bf16[1,16,16,2048]{3,2,0,1:T(8,128)(2,1)S(1)}, u32[]{:S(2)}, u32[]{:S(2)}) %all-to-all-start.1) | async-done | bytes 1048608 | tf_op jit(solution)/shard_map/all_to_all | solution.py:85
  165.6 1.6 copy.63
  167.1 9.7 %bitcast_convert_fusion = (f32[1,256,16,128]{1,3,2,0:T(8,128)}, bf16[16,128,256]{2,1,0:T(8,128)(2,1)S(1)}) fusion(f32[16,768,256]{2,1,0:T(8,128)} %copy-done, f32[16,256]{1,0:T(8,128)S(1)} %log_add_fusion, pred[256,768]{0,1:T(8,128)(4,1)S(1)} %add_bitcast_fusion, bf16[1,256,16,128]{1,3,2,0:T(8,128)(2,1)} %copy.63, ...), kind=kOutput, calls=%fused_computation.37 | convolution fusion | flops 828375040 | bytes 19087360 | tf_op jit(solution)/shard_map/bhij,bjhd->bihd/dot_general | solution.py:111
  176.8 2.3 copy.72
  179.5 1.6 multiply_reduce_fusion.1
  181.0 2.6 all-reduce
  183.7 3.0 fusion.5
  186.9 1.6 bitcast_convert_fusion.1
  188.5 1.9 copy.101
  190.4 1.5 multiply_reduce_fusion
  192.7 8.4 %convolution_convert_fusion = bf16[16,128,768]{2,1,0:T(8,128)(2,1)S(1)} fusion(bf16[256,16,128]{0,2,1:T(8,128)(2,1)S(1)} %copy.87, f32[16,768,256]{2,1,0:T(8,128)} %copy-done, f32[16,256]{1,0:T(8,128)S(1)} %log_add_fusion, pred[256,768]{0,1:T(8,128)(4,1)S(1)} %add_bitcast_fusion), kind=kOutput, calls=%fused_computation.14 | convolution fusion | flops 819462144 | bytes 16990208 | tf_op jit(solution)/shard_map/bhij,bihd->bjhd/dot_general | solution.py:145
  201.1 1.6 fusion.26
  204.1 7.1 %all-to-all-start.6 = ((bf16[1,16,16,2048]{3,2,0,1:T(8,128)(2,1)}), bf16[1,16,16,2048]{3,2,0,1:T(8,128)(2,1)S(1)}, u32[]{:S(2)}, u32[]{:S(2)}) async-start(bf16[1,16,16,2048]{3,2,0,1:T(8,128)(2,1)} %bitcast.60), calls=%async_computation.6 | async-start | bytes 2097152 | tf_op jit(solution)/shard_map/all_to_all | solution.py:158
  211.3 8.9 %multiply_convert_fusion = bf16[16,256,768]{1,2,0:T(8,128)(2,1)S(1)} fusion(f32[16,768,256]{2,1,0:T(8,128)} %copy-done, f32[16,256]{1,0:T(8,128)S(1)} %bitcast.186, f32[16,256]{1,0:T(8,128)S(1)} %log_add_fusion, pred[256,768]{0,1:T(8,128)(4,1)S(1)} %add_bitcast_fusion, bf16[256,16,128]{0,2,1:T(8,128)(2,1)} %copy-done.13, ...), kind=kOutput, calls=%fused_computation.6 | convolution fusion | flops 833617920 | bytes 23298048 | tf_op jit(solution)/shard_map/bihd,bjhd->bhij/dot_general | solution.py:127
  220.2 2.2 multiply_convert_fusion.1
  222.4 1.5 fusion.27
  225.3 10.7 %all-to-all-done.6 = bf16[1,16,16,2048]{3,2,0,1:T(8,128)(2,1)S(1)} async-done(((bf16[1,16,16,2048]{3,2,0,1:T(8,128)(2,1)}), bf16[1,16,16,2048]{3,2,0,1:T(8,128)(2,1)S(1)}, u32[]{:S(2)}, u32[]{:S(2)}) %all-to-all-start.6) | async-done | bytes 1048608 | tf_op jit(solution)/shard_map/all_to_all | solution.py:158
  236.1 6.0 %all-to-all-start.4 = ((bf16[1,16,16,2048]{3,2,0,1:T(8,128)(2,1)}), bf16[1,16,16,2048]{3,2,0,1:T(8,128)(2,1)S(1)}, u32[]{:S(2)}, u32[]{:S(2)}) async-start(bf16[1,16,16,2048]{3,2,0,1:T(8,128)(2,1)} %bitcast.44), calls=%async_computation.4 | async-start | bytes 2097152 | tf_op jit(solution)/shard_map/all_to_all | solution.py:151
  243.4 22.0 %all-to-all-done.4 = bf16[1,16,16,2048]{3,2,0,1:T(8,128)(2,1)S(1)} async-done(((bf16[1,16,16,2048]{3,2,0,1:T(8,128)(2,1)}), bf16[1,16,16,2048]{3,2,0,1:T(8,128)(2,1)S(1)}, u32[]{:S(2)}, u32[]{:S(2)}) %all-to-all-start.4) | async-done | bytes 1048608 | tf_op jit(solution)/shard_map/all_to_all | solution.py:151
  267.3 28.6 %all_to_all.41 = bf16[1,16,16,2048]{3,2,0,1:T(8,128)(2,1)} all-to-all(bf16[1,16,16,2048]{3,2,0,1:T(8,128)(2,1)S(1)} %get-tuple-element.30), channel_id=1, replica_groups=mesh['ctx'=16,'head'=2] {'ctx'}, dimensions={1} | all-to-all | bytes 2097152 | tf_op jit(solution)/shard_map/all_to_all | solution.py:167
  295.9 6.5 %all-to-all-start.7 = ((bf16[1,16,16,2048]{3,2,0,1:T(8,128)(2,1)}), bf16[1,16,16,2048]{3,2,0,1:T(8,128)(2,1)}, u32[]{:S(2)}, u32[]{:S(2)}) async-start(bf16[1,16,16,2048]{3,2,0,1:T(8,128)(2,1)} %get-tuple-element.29), calls=%async_computation.7 | async-start | bytes 2097152 | tf_op jit(solution)/shard_map/all_to_all | solution.py:174
  302.4 2.3 copy.107
  304.7 2.5 collective-permute-start.2
  308.6 3.5 collective-permute-start.3
  312.1 5.9 %multiply_convert_fusion.2 = bf16[16,128,256]{2,1,0:T(8,128)(2,1)} fusion(bf16[16,256,768]{1,2,0:T(8,128)(2,1)} %copy-done.1, bf16[1,256,16,128]{3,1,2,0:T(8,128)(2,1)} %copy-done.10, bf16[1,256,16,128]{3,1,2,0:T(8,128)(2,1)} %copy.68, bf16[1,256,16,128]{3,1,2,0:T(8,128)(2,1)} %copy.67), kind=kOutput, calls=%fused_computation.22 | convolution fusion | flops 815792128 | bytes 10485760 | tf_op jit(solution)/shard_map/bhij,bjhd->bihd/dot_general | solution.py:133
  318.0 2.4 copy.94
  322.4 25.9 %collective-permute-done.2 = bf16[256,2048]{1,0:T(8,128)(2,1)} collective-permute-done((bf16[256,2048]{1,0:T(8,128)(2,1)}, bf16[256,2048]{1,0:T(8,128)(2,1)}, u32[]{:S(2)}, u32[]{:S(2)}) %collective-permute-start.2) | collective-permute-done | bytes 1048608 | tf_op jit(solution)/shard_map/ppermute | solution.py:19
  348.3 3.1 fusion.6
  351.4 18.3 %collective-permute-done.3 = bf16[256,2048]{1,0:T(8,128)(2,1)} collective-permute-done((bf16[256,2048]{1,0:T(8,128)(2,1)}, bf16[256,2048]{1,0:T(8,128)(2,1)}, u32[]{:S(2)}, u32[]{:S(2)}) %collective-permute-start.3) | collective-permute-done | bytes 1048608 | tf_op jit(solution)/shard_map/ppermute | solution.py:19
  369.7 3.1 fusion.7
  (67 shorter events, 17.2 us)
Async XLA Ops:
  32.0 29.7 %all-to-all-start = ((bf16[1,16,16,2048]{3,2,0,1:T(8,128)(2,1)}), bf16[1,16,16,2048]{3,2,0,1:T(8,128)(2,1)S(1)}, u32[]{:S(2)}, u32[]{:S(2)}) async-start(bf16[1,16,16,2048]{3,2,0,1:T(8,128)(2,1)} %bitcast.172), calls=%async_computation | async-start | bytes 2097152 | tf_op jit(solution)/shard_map/all_to_all | solution.py:72
  62.3 7.4 %copy-start.5 = (bf16[256,2048]{1,0:T(8,128)(2,1)S(1)}, bf16[256,2048]{1,0:T(8,128)(2,1)}, u32[]{:S(2)}) copy-start(bf16[256,2048]{1,0:T(8,128)(2,1)} %param.9) | copy-start | bytes 3145732
  63.9 28.9 %all-to-all-start.3 = ((bf16[1,16,16,2048]{3,2,0,1:T(8,128)(2,1)}), bf16[1,16,16,2048]{3,2,0,1:T(8,128)(2,1)S(1)}, u32[]{:S(2)}, u32[]{:S(2)}) async-start(bf16[1,16,16,2048]{3,2,0,1:T(8,128)(2,1)} %get-tuple-element.31), calls=%async_computation.3 | async-start | bytes 2097152 | tf_op jit(solution)/shard_map/all_to_all | solution.py:78
  71.1 48.8 %collective-permute-start.1 = (bf16[256,2048]{0,1:T(8,128)(2,1)}, bf16[256,2048]{0,1:T(8,128)(2,1)}, u32[]{:S(2)}, u32[]{:S(2)}) collective-permute-start(bf16[256,2048]{0,1:T(8,128)(2,1)} %copy.64), channel_id=1, source_target_pairs={{0,2},{2,4},{4,6},{6,8},{8,10},{10,12},{12,14},{14,16},{16,18},{18... | collective-permute-start | bytes 3145736 | tf_op jit(solution)/shard_map/ppermute | solution.py:19
  74.4 72.2 %collective-permute-start = (bf16[256,2048]{1,0:T(8,128)(2,1)}, bf16[256,2048]{1,0:T(8,128)(2,1)}, u32[]{:S(2)}, u32[]{:S(2)}) collective-permute-start(bf16[256,2048]{1,0:T(8,128)(2,1)} %param.10), channel_id=1, source_target_pairs={{0,2},{2,4},{4,6},{6,8},{8,10},{10,12},{12,14},{14,16},{16,18},{18... | collective-permute-start | bytes 3145736 | tf_op jit(solution)/shard_map/ppermute | solution.py:19
  81.6 67.8 %copy-start.2 = (bf16[256,2048]{0,1:T(8,128)(2,1)}, bf16[256,2048]{0,1:T(8,128)(2,1)S(1)}, u32[]{:S(2)}) copy-start(bf16[256,2048]{0,1:T(8,128)(2,1)S(1)} %copy.112) | copy-start | bytes 3145732
  92.8 72.5 %all-to-all-start.1 = ((bf16[1,16,16,2048]{3,2,0,1:T(8,128)(2,1)}), bf16[1,16,16,2048]{3,2,0,1:T(8,128)(2,1)S(1)}, u32[]{:S(2)}, u32[]{:S(2)}) async-start(bf16[1,16,16,2048]{3,2,0,1:T(8,128)(2,1)} %get-tuple-element.32), calls=%async_computation.1 | async-start | bytes 2097152 | tf_op jit(solution)/shard_map/all_to_all | solution.py:85
  149.4 3.7 copy-start.10
  153.1 4.5 %copy-start = (f32[16,768,256]{2,1,0:T(8,128)}, f32[16,768,256]{2,1,0:T(8,128)S(1)}, u32[]{:S(2)}) copy-start(f32[16,768,256]{2,1,0:T(8,128)S(1)} %get-tuple-element.34) | copy-start | bytes 37748740
  153.2 14.0 %copy-start.11 = (bf16[256,2048]{0,1:T(8,128)(2,1)S(1)}, bf16[256,2048]{0,1:T(8,128)(2,1)}, u32[]{:S(2)}) copy-start(bf16[256,2048]{0,1:T(8,128)(2,1)} %copy.61) | copy-start | bytes 3145732
  167.1 12.3 %copy-start.14 = (f32[2048]{0:T(1024)S(1)}, f32[2048]{0:T(1024)}, u32[]{:S(2)}) copy-start(f32[2048]{0:T(1024)} %param.12) | copy-start | bytes 24580
  176.8 9.8 %copy-start.4 = (bf16[16,128,256]{2,1,0:T(8,128)(2,1)}, bf16[16,128,256]{2,1,0:T(8,128)(2,1)S(1)}, u32[]{:S(2)}) copy-start(bf16[16,128,256]{2,1,0:T(8,128)(2,1)S(1)} %get-tuple-element.36) | copy-start | bytes 3145732
  192.7 8.4 %copy-start.13 = (bf16[256,16,128]{0,2,1:T(8,128)(2,1)}, bf16[256,16,128]{0,2,1:T(8,128)(2,1)S(1)}, u32[]{:S(2)}) copy-start(bf16[256,16,128]{0,2,1:T(8,128)(2,1)S(1)} %copy.87) | copy-start | bytes 3145732
  201.1 10.2 %copy-start.12 = (bf16[256,2048]{0,1:T(8,128)(2,1)S(1)}, bf16[256,2048]{0,1:T(8,128)(2,1)}, u32[]{:S(2)}) copy-start(bf16[256,2048]{0,1:T(8,128)(2,1)} %copy.61) | copy-start | bytes 3145732
  204.1 31.9 %all-to-all-start.6 = ((bf16[1,16,16,2048]{3,2,0,1:T(8,128)(2,1)}), bf16[1,16,16,2048]{3,2,0,1:T(8,128)(2,1)S(1)}, u32[]{:S(2)}, u32[]{:S(2)}) async-start(bf16[1,16,16,2048]{3,2,0,1:T(8,128)(2,1)} %bitcast.60), calls=%async_computation.6 | async-start | bytes 2097152 | tf_op jit(solution)/shard_map/all_to_all | solution.py:158
  211.3 8.9 %copy-start.3 = (bf16[256,2048]{0,1:T(8,128)(2,1)S(1)}, bf16[256,2048]{0,1:T(8,128)(2,1)}, u32[]{:S(2)}) copy-start(bf16[256,2048]{0,1:T(8,128)(2,1)} %copy-done.2) | copy-start | bytes 3145732
  220.2 3.7 %copy-start.1 = (bf16[16,256,768]{1,2,0:T(8,128)(2,1)}, bf16[16,256,768]{1,2,0:T(8,128)(2,1)S(1)}, u32[]{:S(2)}) copy-start(bf16[16,256,768]{1,2,0:T(8,128)(2,1)S(1)} %multiply_convert_fusion) | copy-start | bytes 18874372
  222.4 19.7 %copy-start.15 = (s32[16]{0:T(128)S(1)}, s32[16]{0:T(128)}, u32[]{:S(2)}) copy-start(s32[16]{0:T(128)} %param.13) | copy-start | bytes 196
  236.1 29.4 %all-to-all-start.4 = ((bf16[1,16,16,2048]{3,2,0,1:T(8,128)(2,1)}), bf16[1,16,16,2048]{3,2,0,1:T(8,128)(2,1)S(1)}, u32[]{:S(2)}, u32[]{:S(2)}) async-start(bf16[1,16,16,2048]{3,2,0,1:T(8,128)(2,1)} %bitcast.44), calls=%async_computation.4 | async-start | bytes 2097152 | tf_op jit(solution)/shard_map/all_to_all | solution.py:151
  266.0 41.1 %copy-start.7 = (bf16[1,256,2048]{1,2,0:T(8,128)(2,1)S(1)}, bf16[1,256,2048]{1,2,0:T(8,128)(2,1)}, u32[]{:S(2)}) copy-start(bf16[1,256,2048]{1,2,0:T(8,128)(2,1)} %get-tuple-element.19) | copy-start | bytes 3145732
  295.9 73.9 %all-to-all-start.7 = ((bf16[1,16,16,2048]{3,2,0,1:T(8,128)(2,1)}), bf16[1,16,16,2048]{3,2,0,1:T(8,128)(2,1)}, u32[]{:S(2)}, u32[]{:S(2)}) async-start(bf16[1,16,16,2048]{3,2,0,1:T(8,128)(2,1)} %get-tuple-element.29), calls=%async_computation.7 | async-start | bytes 2097152 | tf_op jit(solution)/shard_map/all_to_all | solution.py:174
  304.7 43.6 %collective-permute-start.2 = (bf16[256,2048]{1,0:T(8,128)(2,1)}, bf16[256,2048]{1,0:T(8,128)(2,1)}, u32[]{:S(2)}, u32[]{:S(2)}) collective-permute-start(bf16[256,2048]{1,0:T(8,128)(2,1)} %bitcast.39), channel_id=1, source_target_pairs={{2,0},{4,2},{6,4},{8,6},{10,8},{12,10},{14,12},{16,14},{18,16},{20... | collective-permute-start | bytes 3145736 | tf_op jit(solution)/shard_map/ppermute | solution.py:19
  308.6 11.8 %copy-start.8 = (bf16[1,256,2048]{1,2,0:T(8,128)(2,1)S(1)}, bf16[1,256,2048]{1,2,0:T(8,128)(2,1)}, u32[]{:S(2)}) copy-start(bf16[1,256,2048]{1,2,0:T(8,128)(2,1)} %get-tuple-element.23) | copy-start | bytes 3145732
  308.6 13.2 %copy-start.6 = (bf16[1,256,2048]{1,2,0:T(8,128)(2,1)S(1)}, bf16[1,256,2048]{1,2,0:T(8,128)(2,1)}, u32[]{:S(2)}) copy-start(bf16[1,256,2048]{1,2,0:T(8,128)(2,1)} %get-tuple-element.20) | copy-start | bytes 3145732
  308.6 61.1 %collective-permute-start.3 = (bf16[256,2048]{1,0:T(8,128)(2,1)}, bf16[256,2048]{1,0:T(8,128)(2,1)}, u32[]{:S(2)}, u32[]{:S(2)}) collective-permute-start(bf16[256,2048]{1,0:T(8,128)(2,1)} %bitcast.184), channel_id=1, source_target_pairs={{2,0},{4,2},{6,4},{8,6},{10,8},{12,10},{14,12},{16,14},{18,16},{20... | collective-permute-start | bytes 3145736 | tf_op jit(solution)/shard_map/ppermute | solution.py:19
  318.0 30.3 %copy-start.9 = (bf16[1,16,16,2048]{3,2,0,1:T(8,128)(2,1)S(1)}, bf16[1,16,16,2048]{3,2,0,1:T(8,128)(2,1)}, u32[]{:S(2)}) copy-start(bf16[1,16,16,2048]{3,2,0,1:T(8,128)(2,1)} %all_to_all.41) | copy-start | bytes 3145732
where the time goes:
time: 374 us; the launch traced here: 373 us
  waiting for transfers between devices  159 us (43%)
  blocking collectives  62.6 us (17%)
  starting transfers between devices  51.6 us (14%)
  local copies, waits for them, and re-layouts  39 us (10%)
  matrix products  38.7 us (10%)
  other arithmetic  21.1 us (6%)
    ppermute x4, waiting for transfers between devices, from_behind(): lax.ppermute(value, axis, [(source, source + steps) for source in range(f...  88.2 us
    all_to_all x1, blocking collectives, on_device(): lax.all_to_all(spread_rows(key_blocks, devices), 'ctx', split_axis=1, con...  31.4 us
    all_to_all x1, blocking collectives, on_device(): lax.all_to_all(choose_pieces(returned[0], inverse, devices), 'ctx', split...  28.6 us
    all_to_all x1, waiting for transfers between devices, on_device(): lax.all_to_all(spread_rows(key_terms[:, 2 * BLOCK:], devices), 'ctx', spl...  22 us
    all_to_all x1, waiting for transfers between devices, on_device(): lax.all_to_all(spread_rows(value_blocks, devices), 'ctx', split_axis=1, c...  21.7 us
    unnamed x45, local copies, waits for them, and re-layouts  19.2 us
    ppermute x4, starting transfers between devices, from_behind(): lax.ppermute(value, axis, [(source, source + steps) for source in range(f...  12.7 us
    all_to_all x1, waiting for transfers between devices, on_device(): lax.all_to_all(spread_rows(value_terms[:, 2 * BLOCK:], devices), 'ctx', s...  10.7 us
  transfers between devices with their start and end apart: 10, of which 9 were waited for; matrix products, arithmetic and copies ran while one was open for 14% of the time, Pallas kernels for 0%

commit v1 on v0

v1 whole, which is shorter than its diff:
```python
import functools
import math

import jax
import jax.numpy as jnp
from jax import lax
from jax.experimental import pallas as pl
from jax.experimental.pallas import tpu as pltpu
from jax.sharding import PartitionSpec as P

HEADS = 32
HD = 128
BLOCK = 256
EPSILON = 1e-05
FACTOR = 1.0 / math.sqrt(HD)
LOG2E = math.log2(math.e)
MASKED = -1e30
F32 = jnp.float32
BF16 = jnp.bfloat16


def dot(a, b, contract):
    return lax.dot_general(a, b, (contract, ((), ())), preferred_element_type=F32)


NT = ((1,), (1,))
NN = ((1,), (0,))
TN = ((0,), (0,))


def head(h):
    return pl.ds(h * HD, HD)


def scores_kernel(group, index_ref, q, kp, ko, kt, vp, vo, pp_out, po_out, pt_out, acc_out):
    first = index_ref[0] == 0
    rows = lax.broadcasted_iota(jnp.int32, (BLOCK, BLOCK), 0)
    cols = lax.broadcasted_iota(jnp.int32, (BLOCK, BLOCK), 1)
    causal = rows >= cols
    for h in range(group):
        here = q[:, head(h)]
        scale = FACTOR * LOG2E
        sp = jnp.where(first, MASKED, dot(here, kp[:, head(h)], NT) * scale)
        so = jnp.where(causal, dot(here, ko[:, head(h)], NT) * scale, MASKED)
        st = dot(here, kt[:, head(h)], NT) * scale
        top = jnp.max(jnp.maximum(jnp.maximum(sp, so), st), axis=1, keepdims=True)
        ep = jnp.exp2(sp - top)
        eo = jnp.exp2(so - top)
        et = jnp.exp2(st - top)
        inverse = 1.0 / jnp.sum(ep + eo + et, axis=1, keepdims=True)
        wp = (ep * inverse).astype(BF16)
        wo = (eo * inverse).astype(BF16)
        pp_out[h] = wp
        po_out[h] = wo
        pt_out[h] = (et * inverse).astype(BF16)
        acc_out[:, head(h)] = dot(wp, vp[:, head(h)], NN) + dot(wo, vo[:, head(h)], NN)


def attn_kernel(group, steps, pt, vt, acc, cot, gain, attn_out, sums_out, square, product):
    step = pl.program_id(0)

    @pl.when(step == 0)
    def _():
        square[...] = jnp.zeros_like(square)
        product[...] = jnp.zeros_like(product)

    sq = square[...]
    pr = product[...]
    for h in range(group):
        low = (acc[:, head(h)] + dot(pt[h], vt[:, head(h)], NN)).astype(BF16)
        attn_out[:, head(h)] = low
        wide = low.astype(F32)
        sq = sq + wide * wide
        pr = pr + gain[:, head(h)] * cot[:, head(h)].astype(F32) * wide
    square[...] = sq
    product[...] = pr

    @pl.when(step == steps - 1)
    def _():
        sums_out[0:1, :] = jnp.sum(jnp.transpose(square[...]), axis=0, keepdims=True)
        sums_out[1:2, :] = jnp.sum(jnp.transpose(product[...]), axis=0, keepdims=True)


def norm_terms(sums, features):
    table = jnp.concatenate([sums[...], jnp.zeros((6, BLOCK), F32)], axis=0)
    columns = jnp.transpose(table)
    rms = lax.rsqrt(columns[:, 0:1] / features + EPSILON)
    return rms, columns[:, 1:2] / features


def dattn_kernel(group, features, sums, attn, cot, gain, pt, dattn_out, dvt_out):
    rms, mean = norm_terms(sums, features)
    back = rms * rms * rms * mean
    for h in range(group):
        grad_in = gain[:, head(h)] * cot[:, head(h)].astype(F32)
        low = (rms * grad_in - attn[:, head(h)].astype(F32) * back).astype(BF16)
        dattn_out[:, head(h)] = low
        dvt_out[:, head(h)] = dot(pt[h], low, TN).astype(BF16)


def dscore_of(weights, dattn, attn, values):
    delta = jnp.sum(dattn.astype(F32) * attn.astype(F32), axis=1, keepdims=True)
    return (weights.astype(F32) * (dot(dattn, values, NT) - delta)).astype(BF16)


def partner_kernel(group, pt, dattn, attn, vt, kt, q, dkt_out, dq_out):
    for h in range(group):
        ds = dscore_of(pt[h], dattn[:, head(h)], attn[:, head(h)], vt[:, head(h)])
        dkt_out[:, head(h)] = (dot(ds, q[:, head(h)], TN) * FACTOR).astype(BF16)
        dq_out[:, head(h)] = dot(ds, kt[:, head(h)], NN)


def prior_kernel(group, pp, dattn, attn, vp, kp, q, dq_in, dvp_out, dkp_out, dq_out):
    for h in range(group):
        low = dattn[:, head(h)]
        ds = dscore_of(pp[h], low, attn[:, head(h)], vp[:, head(h)])
        dvp_out[:, head(h)] = dot(pp[h], low, TN).astype(BF16)
        dkp_out[:, head(h)] = (dot(ds, q[:, head(h)], TN) * FACTOR).astype(BF16)
        dq_out[:, head(h)] = dq_in[:, head(h)] + dot(ds, kp[:, head(h)], NN)


def own_kernel(group, features, sums, po, dattn, attn, vo, ko, q, dq_in, gain, dvo_out, dko_out, dq_out, mixed_out):
    rms, _ = norm_terms(sums, features)
    for h in range(group):
        low = dattn[:, head(h)]
        ds = dscore_of(po[h], low, attn[:, head(h)], vo[:, head(h)])
        dvo_out[:, head(h)] = dot(po[h], low, TN).astype(BF16)
        dko_out[:, head(h)] = (dot(ds, q[:, head(h)], TN) * FACTOR).astype(BF16)
        dq_out[:, head(h)] = ((dq_in[:, head(h)] + dot(ds, ko[:, head(h)], NN)) * FACTOR).astype(BF16)
        mixed_out[:, head(h)] = (attn[:, head(h)].astype(F32) * rms * gain[:, head(h)]).astype(BF16)


def from_behind(value, steps):
    count = lax.axis_size("ctx")
    first, last = (max(0, -steps), min(count, count - steps))
    return lax.ppermute(value, "ctx", [(source, source + steps) for source in range(first, last)])


def exchange(pieces):
    return lax.all_to_all(pieces, "ctx", split_axis=0, concat_axis=0, tiled=True)


def spread(value):
    devices = lax.axis_size("ctx")
    return exchange(value.reshape(devices, value.shape[0] // devices, value.shape[1]))


def collect(pieces, wanted):
    chosen = jnp.take(pieces, wanted, axis=0, mode="clip")
    return exchange(chosen).reshape(pieces.shape[0] * pieces.shape[1], pieces.shape[2])


def on_device(queries, key_rows, value_rows, cotangent, norm_gain, pairing):
    width = queries.shape[1]
    heads = width // HD
    group = math.gcd(4, heads)
    steps = heads // group
    features = float(HEADS * HD)
    wide = pl.BlockSpec((BLOCK, group * HD), lambda g: (0, g))
    square = pl.BlockSpec((group, BLOCK, BLOCK), lambda g: (g, 0, 0))
    line = pl.BlockSpec((1, group * HD), lambda g: (0, g))
    whole = pl.BlockSpec((2, BLOCK), lambda g: (0, 0))
    rows_low = jax.ShapeDtypeStruct((BLOCK, width), BF16)
    rows_wide = jax.ShapeDtypeStruct((BLOCK, width), F32)
    weights = jax.ShapeDtypeStruct((heads, BLOCK, BLOCK), BF16)

    def call(body, name, ins, outs, shapes, dots, exps=0, scratch=()):
        return pl.pallas_call(
            body,
            name=name,
            grid=(steps,),
            in_specs=ins,
            out_specs=outs,
            out_shape=shapes,
            scratch_shapes=scratch,
            compiler_params=pltpu.CompilerParams(vmem_limit_bytes=32 * 2**20),
            cost_estimate=pl.CostEstimate(
                flops=dots * heads * 2 * BLOCK * BLOCK * HD,
                bytes_accessed=(len(ins) + len(outs)) * BLOCK * width * 2,
                transcendentals=exps * heads * BLOCK * BLOCK,
            ),
        )

    gain = norm_gain.reshape(1, width)
    index = lax.axis_index("ctx").astype(jnp.int32).reshape(1)
    numbers = jnp.arange(pairing.shape[0], dtype=jnp.int32)
    inverse = jnp.sum(
        jnp.where(pairing[None, :] == numbers[:, None], numbers[None, :], 0), axis=1
    )

    kp = from_behind(key_rows, 1)
    vp = from_behind(value_rows, 1)
    keys_spread = spread(key_rows)
    values_spread = spread(value_rows)
    kt = collect(keys_spread, pairing)
    vt = collect(values_spread, pairing)

    smem = pl.BlockSpec(memory_space=pltpu.SMEM)
    pp, po, pt, acc = call(
        functools.partial(scores_kernel, group),
        "scores",
        [smem] + [wide] * 6,
        [square] * 3 + [wide],
        [weights] * 3 + [rows_wide],
        5,
        3,
    )(index, queries, kp, key_rows, kt, vp, value_rows)
    attn, sums = call(
        functools.partial(attn_kernel, group, steps),
        "attn",
        [square, wide, wide, wide, line],
        [wide, whole],
        [rows_low, jax.ShapeDtypeStruct((2, BLOCK), F32)],
        1,
        scratch=[pltpu.VMEM((BLOCK, HD), F32)] * 2,
    )(pt, vt, acc, cotangent, gain)
    sums = lax.psum(sums, "head")
    dattn, dvt = call(
        functools.partial(dattn_kernel, group, features),
        "dattn",
        [whole, wide, wide, line, square],
        [wide, wide],
        [rows_low] * 2,
        1,
    )(sums, attn, cotangent, gain, pt)
    dvt_spread = spread(dvt)
    dkt, dq = call(
        functools.partial(partner_kernel, group),
        "partner",
        [square] + [wide] * 5,
        [wide, wide],
        [rows_low, rows_wide],
        3,
    )(pt, dattn, attn, vt, kt, queries)
    dkt_spread = spread(dkt)
    dvp, dkp, dq = call(
        functools.partial(prior_kernel, group),
        "prior",
        [square] + [wide] * 6,
        [wide] * 3,
        [rows_low, rows_low, rows_wide],
        4,
    )(pp, dattn, attn, vp, kp, queries, dq)
    dvn = from_behind(dvp, -1)
    dkn = from_behind(dkp, -1)
    dvo, dko, grad_query, mixed = call(
        functools.partial(own_kernel, group, features),
        "own",
        [whole, square] + [wide] * 6 + [line],
        [wide] * 4,
        [rows_low] * 4,
        4,
    )(sums, po, dattn, attn, value_rows, key_rows, queries, dq, gain)
    dvt_home = collect(dvt_spread, inverse)
    dkt_home = collect(dkt_spread, inverse)
    grad_value = (dvo.astype(F32) + dvn.astype(F32) + dvt_home.astype(F32)).astype(BF16)
    grad_key = (dko.astype(F32) + dkn.astype(F32) + dkt_home.astype(F32)).astype(BF16)
    return mixed, grad_query, grad_key, grad_value


def solution(mesh):
    rows = P("ctx", "head")
    return jax.shard_map(
        on_device,
        mesh=mesh,
        in_specs=(rows, rows, rows, rows, P("head"), P()),
        out_specs=(rows, rows, rows, rows),
        check_vma=False,
    )
```

time: 374 us -> 373 us (level)
  matrix products: 38.7 us -> 0 us
  Pallas kernels: 0 us -> 38.3 us
  waiting for transfers between devices: 159 us -> 184 us
  other arithmetic: 21.1 us -> 6.32 us
  local copies, waits for them, and re-layouts: 39 us -> 28.4 us
    dot_general x6 -> x0, matrix products: 38.7 us -> none  [the longest x1 9.71 us: on_device(): jnp.einsum('bhij,bjhd->bihd', weights_low, values_window, preferred_eleme...]
    pallas_call x0 -> x6, Pallas kernels: none -> 38.3 us  [the longest x1 10.1 us: on_device(): call(functools.partial(scores_kernel, group), 'scores', [smem] + [wide] *...]
    all_to_all x6, waiting for transfers between devices: 70.6 us -> 84.3 us  [exchange(): lax.all_to_all(pieces, 'ctx', split_axis=0, concat_axis=0, tiled=True)]
    ppermute x4, waiting for transfers between devices: 88.2 us -> 99.9 us  [from_behind(): lax.ppermute(value, 'ctx', [(source, source + steps) for source in range(...]
    concatenate x6 -> x0, local copies, waits for them, and re-layouts: 6.77 us -> none  [the longest x3 5.19 us: on_device(): jnp.concatenate([prior_keys, key_blocks, partner_keys], axis=1)]
    gather x4, local copies, waits for them, and re-layouts: 2.45 us -> 9.08 us  [collect(): chosen = jnp.take(pieces, wanted, axis=0, mode='clip')]
    convert_element_type x0 -> x2, other arithmetic: none -> 6.19 us  [the longest x1 3.41 us: on_device(): (dvo.astype(F32) + dvn.astype(F32) + dvt_home.astype(F32)).astype(BF16)]
    reshape x2 -> x0, other arithmetic: 6.11 us -> none  [the longest x1 3.06 us: on_device(): grad_key.reshape(rows_here, width)]
  transfers between devices with their start and end apart: 10 -> 10, of which waited for: 9 -> 8; matrix products, arithmetic and copies ran while one was open for 14% -> 3% of each run, Pallas kernels for 0% -> 7%
where the time goes in v1:
time: 373 us; the launch traced here: 371 us
  waiting for transfers between devices  184 us (49%)
  blocking collectives  65.3 us (18%)
  starting transfers between devices  48.2 us (13%)
  Pallas kernels  38.3 us (10%)
  local copies, waits for them, and re-layouts  28.4 us (8%)
  other arithmetic  6.32 us (2%)
    ppermute x4, waiting for transfers between devices, from_behind(): lax.ppermute(value, 'ctx', [(source, source + steps) for source in range(...  99.9 us
    all_to_all x6, waiting for transfers between devices, exchange(): lax.all_to_all(pieces, 'ctx', split_axis=0, concat_axis=0, tiled=True)  84.3 us
    all_to_all x2, blocking collectives, exchange(): lax.all_to_all(pieces, 'ctx', split_axis=0, concat_axis=0, tiled=True)  62.8 us
    all_to_all x6, starting transfers between devices, exchange(): lax.all_to_all(pieces, 'ctx', split_axis=0, concat_axis=0, tiled=True)  35.6 us
    unnamed x56, local copies, waits for them, and re-layouts  19.3 us
    ppermute x4, starting transfers between devices, from_behind(): lax.ppermute(value, 'ctx', [(source, source + steps) for source in range(...  12.6 us
    pallas_call x1, Pallas kernels, on_device(): call(functools.partial(scores_kernel, group), 'scores', [smem] + [wide] *...  10.1 us
    gather x4, local copies, waits for them, and re-layouts, collect(): chosen = jnp.take(pieces, wanted, axis=0, mode='clip')  9.08 us
  transfers between devices with their start and end apart: 10, of which 8 were waited for; matrix products, arithmetic and copies ran while one was open for 3% of the time, Pallas kernels for 7%

profile of v1, /device:TPU:14, one launch (start us, length us, event | category | flops | bytes accessed | tf_op | source)
XLA Modules:
  0.0 371.4 jit_solution(18441683847359572847)
XLA Ops:
  0.6 31.4 %all_to_all.40 = bf16[16,16,2048]{2,1,0:T(8,128)(2,1)S(1)} all-to-all(bf16[16,16,2048]{2,1,0:T(8,128)(2,1)} %bitcast.14), channel_id=1, replica_groups=mesh['ctx'=16,'head'=2] {'ctx'}, dimensions={0} | all-to-all | bytes 2097152 | tf_op jit(solution)/shard_map/all_to_all | solution.py:140
  32.0 6.0 %all-to-all-start.2 = ((bf16[16,16,2048]{2,1,0:T(8,128)(2,1)}), bf16[16,16,2048]{2,1,0:T(8,128)(2,1)S(1)}, u32[]{:S(2)}, u32[]{:S(2)}) async-start(bf16[16,16,2048]{2,1,0:T(8,128)(2,1)} %bitcast.3), calls=%async_computation.2 | async-start | bytes 2097152 | tf_op jit(solution)/shard_map/all_to_all | solution.py:140
  38.1 1.6 gather_fusion
  39.7 22.1 %all-to-all-done.2 = bf16[16,16,2048]{2,1,0:T(8,128)(2,1)S(1)} async-done(((bf16[16,16,2048]{2,1,0:T(8,128)(2,1)}), bf16[16,16,2048]{2,1,0:T(8,128)(2,1)S(1)}, u32[]{:S(2)}, u32[]{:S(2)}) %all-to-all-start.2) | async-done | bytes 1048608 | tf_op jit(solution)/shard_map/all_to_all | solution.py:140
  61.7 1.0 copy-done.26
  62.7 5.8 %all-to-all-start.1 = ((bf16[16,16,2048]{2,1,0:T(8,128)(2,1)}), bf16[16,16,2048]{2,1,0:T(8,128)(2,1)S(1)}, u32[]{:S(2)}, u32[]{:S(2)}) async-start(bf16[16,16,2048]{2,1,0:T(8,128)(2,1)} %gather_fusion), calls=%async_computation.1 | async-start | bytes 2097152 | tf_op jit(solution)/shard_map/all_to_all | solution.py:140
  68.6 3.0 gather_fusion.1
  71.5 20.0 %all-to-all-done.1 = bf16[16,16,2048]{2,1,0:T(8,128)(2,1)S(1)} async-done(((bf16[16,16,2048]{2,1,0:T(8,128)(2,1)}), bf16[16,16,2048]{2,1,0:T(8,128)(2,1)S(1)}, u32[]{:S(2)}, u32[]{:S(2)}) %all-to-all-start.1) | async-done | bytes 1048608 | tf_op jit(solution)/shard_map/all_to_all | solution.py:140
  91.5 6.0 %all-to-all-start.3 = ((bf16[16,16,2048]{2,1,0:T(8,128)(2,1)}), bf16[16,16,2048]{2,1,0:T(8,128)(2,1)}, u32[]{:S(2)}, u32[]{:S(2)}) async-start(bf16[16,16,2048]{2,1,0:T(8,128)(2,1)} %gather_fusion.1), calls=%async_computation.3 | async-start | bytes 2097152 | tf_op jit(solution)/shard_map/all_to_all | solution.py:140
  97.5 3.4 collective-permute-start
  100.9 3.4 collective-permute-start.1
  104.3 37.4 %collective-permute-done.kp = bf16[256,2048]{1,0:T(8,128)(2,1)} collective-permute-done((bf16[256,2048]{1,0:T(8,128)(2,1)S(1)}, bf16[256,2048]{1,0:T(8,128)(2,1)}, u32[]{:S(2)}, u32[]{:S(2)}) %collective-permute-start) | collective-permute-done | bytes 1048608 | tf_op jit(solution)/shard_map/ppermute | solution.py:136
  141.7 21.7 %collective-permute-done.1.vp = bf16[256,2048]{1,0:T(8,128)(2,1)} collective-permute-done((bf16[256,2048]{1,0:T(8,128)(2,1)}, bf16[256,2048]{1,0:T(8,128)(2,1)}, u32[]{:S(2)}, u32[]{:S(2)}) %collective-permute-start.1) | collective-permute-done | bytes 1048608 | tf_op jit(solution)/shard_map/ppermute | solution.py:136
  163.4 1.2 copy-done.8
  164.6 1.2 copy-done.11
  165.8 10.1 %scores.1 = (bf16[16,256,256]{2,1,0:T(8,128)(2,1)S(1)}, bf16[16,256,256]{2,1,0:T(8,128)(2,1)S(1)}, bf16[16,256,256]{2,1,0:T(8,128)(2,1)S(1)}, f32[256,2048]{1,0:T(8,128)S(1)}) custom-call(s32[1]{0:T(128)} %bitcast.index_ref, bf16[256,2048]{1,0:T(8,128)(2,1)S(1)} %copy-done, bf16[256,2048]{1,0:T(8,128)(2,1)} %collective-permute-done.kp, ...), custom_call_target="tpu_custom_call" | custom-call | flops 1342177280 | bytes 11534336 | tf_op jit(solution)/shard_map/scores/pallas_call | solution.py:199
  176.0 1.4 copy-done.15
  177.3 1.4 copy-done.17
  178.7 1.3 copy-done.19
  180.0 1.2 copy-done.13
  181.2 1.6 copy-done.16
  182.8 3.2 attn.1
  186.0 1.0 copy-done.1
  187.0 2.4 psum.7.sums
  189.4 1.2 copy-done.2
  190.7 1.2 copy-done.14
  191.9 3.6 dattn.1
  195.5 6.3 %partner.1 = (bf16[256,2048]{1,0:T(8,128)(2,1)S(1)}, f32[256,2048]{1,0:T(8,128)S(1)}) custom-call(bf16[16,256,256]{2,1,0:T(8,128)(2,1)S(1)} %get-tuple-element.21.pt, bf16[256,2048]{1,0:T(8,128)(2,1)S(1)} %get-tuple-element.26.dattn, bf16[256,2048]{1,0:T(8,128)(2,1)S(1)} %copy-done.3, bf16[256,2048]{1,0:T(8,128)(2,1)} %bitcast.4.vt, ...), custom_call_target="tpu_custom_call" | custom-call | flops 805306368 | bytes 8388608 | tf_op jit(solution)/shard_map/partner/pallas_call | solution.py:227
  201.8 1.4 copy-done.21
  203.2 31.4 %all_to_all.41 = bf16[16,16,2048]{2,1,0:T(8,128)(2,1)S(1)} all-to-all(bf16[16,16,2048]{2,1,0:T(8,128)(2,1)S(1)} %bitcast.17), channel_id=1, replica_groups=mesh['ctx'=16,'head'=2] {'ctx'}, dimensions={0} | all-to-all | bytes 2097152 | tf_op jit(solution)/shard_map/all_to_all | solution.py:140
  234.6 6.0 %all-to-all-start.6 = ((bf16[16,16,2048]{2,1,0:T(8,128)(2,1)}), bf16[16,16,2048]{2,1,0:T(8,128)(2,1)S(1)}, u32[]{:S(2)}, u32[]{:S(2)}) async-start(bf16[16,16,2048]{2,1,0:T(8,128)(2,1)} %bitcast.8), calls=%async_computation.6 | async-start | bytes 2097152 | tf_op jit(solution)/shard_map/all_to_all | solution.py:140
  240.7 1.6 gather_fusion.2
  242.3 22.0 %all-to-all-done.6 = bf16[16,16,2048]{2,1,0:T(8,128)(2,1)S(1)} async-done(((bf16[16,16,2048]{2,1,0:T(8,128)(2,1)}), bf16[16,16,2048]{2,1,0:T(8,128)(2,1)S(1)}, u32[]{:S(2)}, u32[]{:S(2)}) %all-to-all-start.6) | async-done | bytes 1048608 | tf_op jit(solution)/shard_map/all_to_all | solution.py:140
  264.3 1.0 copy-done.25
  265.3 5.8 %all-to-all-start.5 = ((bf16[16,16,2048]{2,1,0:T(8,128)(2,1)}), bf16[16,16,2048]{2,1,0:T(8,128)(2,1)}, u32[]{:S(2)}, u32[]{:S(2)}) async-start(bf16[16,16,2048]{2,1,0:T(8,128)(2,1)} %gather_fusion.2), calls=%async_computation.5 | async-start | bytes 2097152 | tf_op jit(solution)/shard_map/all_to_all | solution.py:140
  271.1 3.0 gather_fusion.3
  274.1 20.2 %all-to-all-done.5 = bf16[16,16,2048]{2,1,0:T(8,128)(2,1)} async-done(((bf16[16,16,2048]{2,1,0:T(8,128)(2,1)}), bf16[16,16,2048]{2,1,0:T(8,128)(2,1)}, u32[]{:S(2)}, u32[]{:S(2)}) %all-to-all-start.5) | async-done | bytes 1048608 | tf_op jit(solution)/shard_map/all_to_all | solution.py:140
  294.3 5.9 %all-to-all-start.7 = ((bf16[16,16,2048]{2,1,0:T(8,128)(2,1)}), bf16[16,16,2048]{2,1,0:T(8,128)(2,1)}, u32[]{:S(2)}, u32[]{:S(2)}) async-start(bf16[16,16,2048]{2,1,0:T(8,128)(2,1)} %gather_fusion.3), calls=%async_computation.7 | async-start | bytes 2097152 | tf_op jit(solution)/shard_map/all_to_all | solution.py:140
  300.2 1.6 copy-done.20
  301.8 1.6 copy-done.22
  303.4 7.2 %prior.1 = (bf16[256,2048]{1,0:T(8,128)(2,1)S(1)}, bf16[256,2048]{1,0:T(8,128)(2,1)S(1)}, f32[256,2048]{1,0:T(8,128)S(1)}) custom-call(bf16[16,256,256]{2,1,0:T(8,128)(2,1)S(1)} %copy-done.20, bf16[256,2048]{1,0:T(8,128)(2,1)S(1)} %copy-done.6, bf16[256,2048]{1,0:T(8,128)(2,1)S(1)} %copy-done.4, bf16[256,2048]{1,0:T(8,128)(2,1)} %collective-permute-done.1.vp, ...), custom_call_target="tpu_custom_call" | custom-call | flops 1073741824 | bytes 10485760 | tf_op jit(solution)/shard_map/prior/pallas_call | solution.py:236
  310.6 2.5 collective-permute-start.2
  313.1 3.4 collective-permute-start.3
  316.5 7.9 %own.1 = (bf16[256,2048]{1,0:T(8,128)(2,1)S(1)}, bf16[256,2048]{1,0:T(8,128)(2,1)S(1)}, bf16[256,2048]{1,0:T(8,128)(2,1)}, bf16[256,2048]{1,0:T(8,128)(2,1)}) custom-call(f32[2,256]{1,0:T(2,128)S(1)} %psum.7.sums, bf16[16,256,256]{2,1,0:T(8,128)(2,1)S(1)} %copy-done.18, bf16[256,2048]{1,0:T(8,128)(2,1)S(1)} %copy-done.6, bf16[256,2048]{1,0:T(8,128)(2,1)S(1)} %copy-done.4, ...), custom_call_target="tpu_custom_call" | custom-call | flops 1073741824 | bytes 13631488 | tf_op jit(solution)/shard_map/own/pallas_call | solution.py:246
  324.4 22.0 %collective-permute-done.2 = bf16[256,2048]{1,0:T(8,128)(2,1)S(1)} collective-permute-done((bf16[256,2048]{1,0:T(8,128)(2,1)S(1)}, bf16[256,2048]{1,0:T(8,128)(2,1)S(1)}, u32[]{:S(2)}, u32[]{:S(2)}) %collective-permute-start.2) | collective-permute-done | bytes 1048608 | tf_op jit(solution)/shard_map/ppermute | solution.py:136
  346.5 2.8 fusion.1
  349.3 18.7 %collective-permute-done.3 = bf16[256,2048]{1,0:T(8,128)(2,1)} collective-permute-done((bf16[256,2048]{1,0:T(8,128)(2,1)S(1)}, bf16[256,2048]{1,0:T(8,128)(2,1)}, u32[]{:S(2)}, u32[]{:S(2)}) %collective-permute-start.3) | collective-permute-done | bytes 1048608 | tf_op jit(solution)/shard_map/ppermute | solution.py:136
  368.0 3.4 fusion
  (46 shorter events, 0.2 us)
Async XLA Ops:
  0.6 37.4 %copy-start.27 = (s32[16]{0:T(128)S(1)}, s32[16]{0:T(128)}, u32[]{:S(2)}) copy-start(s32[16]{0:T(128)} %param.11) | copy-start | bytes 196
  32.0 29.7 %all-to-all-start.2 = ((bf16[16,16,2048]{2,1,0:T(8,128)(2,1)}), bf16[16,16,2048]{2,1,0:T(8,128)(2,1)S(1)}, u32[]{:S(2)}, u32[]{:S(2)}) async-start(bf16[16,16,2048]{2,1,0:T(8,128)(2,1)} %bitcast.3), calls=%async_computation.2 | async-start | bytes 2097152 | tf_op jit(solution)/shard_map/all_to_all | solution.py:140
  61.7 1.0 copy-start.26
  62.7 28.8 %all-to-all-start.1 = ((bf16[16,16,2048]{2,1,0:T(8,128)(2,1)}), bf16[16,16,2048]{2,1,0:T(8,128)(2,1)S(1)}, u32[]{:S(2)}, u32[]{:S(2)}) async-start(bf16[16,16,2048]{2,1,0:T(8,128)(2,1)} %gather_fusion), calls=%async_computation.1 | async-start | bytes 2097152 | tf_op jit(solution)/shard_map/all_to_all | solution.py:140
  68.5 29.0 %copy-start.7 = (bf16[256,2048]{1,0:T(8,128)(2,1)S(1)}, bf16[256,2048]{1,0:T(8,128)(2,1)}, u32[]{:S(2)}) copy-start(bf16[256,2048]{1,0:T(8,128)(2,1)} %ko.3) | copy-start | bytes 3145732
  68.5 94.9 %copy-start = (bf16[256,2048]{1,0:T(8,128)(2,1)S(1)}, bf16[256,2048]{1,0:T(8,128)(2,1)}, u32[]{:S(2)}) copy-start(bf16[256,2048]{1,0:T(8,128)(2,1)} %q.7) | copy-start | bytes 3145732
  91.5 71.9 %copy-start.10 = (bf16[16,16,2048]{2,1,0:T(8,128)(2,1)}, bf16[16,16,2048]{2,1,0:T(8,128)(2,1)S(1)}, u32[]{:S(2)}) copy-start(bf16[16,16,2048]{2,1,0:T(8,128)(2,1)S(1)} %all-to-all-done.1) | copy-start | bytes 3145732
  91.5 88.5 %all-to-all-start.3 = ((bf16[16,16,2048]{2,1,0:T(8,128)(2,1)}), bf16[16,16,2048]{2,1,0:T(8,128)(2,1)}, u32[]{:S(2)}, u32[]{:S(2)}) async-start(bf16[16,16,2048]{2,1,0:T(8,128)(2,1)} %gather_fusion.1), calls=%async_computation.3 | async-start | bytes 2097152 | tf_op jit(solution)/shard_map/all_to_all | solution.py:140
  97.5 44.2 %collective-permute-start = (bf16[256,2048]{1,0:T(8,128)(2,1)S(1)}, bf16[256,2048]{1,0:T(8,128)(2,1)}, u32[]{:S(2)}, u32[]{:S(2)}) collective-permute-start(bf16[256,2048]{1,0:T(8,128)(2,1)S(1)} %copy-done.7), channel_id=1, source_target_pairs={{0,2},{2,4},{4,6},{6,8},{8,10},{10,12},{12,14},{14,16},{16,18},{18... | collective-permute-start | bytes 3145736 | tf_op jit(solution)/shard_map/ppermute | solution.py:136
  100.9 62.5 %collective-permute-start.1 = (bf16[256,2048]{1,0:T(8,128)(2,1)}, bf16[256,2048]{1,0:T(8,128)(2,1)}, u32[]{:S(2)}, u32[]{:S(2)}) collective-permute-start(bf16[256,2048]{1,0:T(8,128)(2,1)} %vo.3), channel_id=1, source_target_pairs={{0,2},{2,4},{4,6},{6,8},{8,10},{10,12},{12,14},{14,16},{16,18},{18... | collective-permute-start | bytes 3145736 | tf_op jit(solution)/shard_map/ppermute | solution.py:136
  163.4 1.2 copy-start.8
  164.6 1.2 copy-start.11
  165.8 14.2 %copy-start.24 = (f32[2048]{0:T(1024)S(1)}, f32[2048]{0:T(1024)}, u32[]{:S(2)}) copy-start(f32[2048]{0:T(1024)} %param.10) | copy-start | bytes 24580
  175.9 1.4 copy-start.15
  177.3 1.4 copy-start.17
  178.7 1.3 copy-start.19
  180.0 1.2 copy-start.13
  181.2 1.6 copy-start.16
  186.0 1.0 copy-start.1
  189.4 1.2 copy-start.2
  190.7 1.2 copy-start.14
  191.9 3.6 copy-start.3
  191.9 3.6 copy-start.12
  195.5 6.3 %copy-start.5 = (bf16[256,2048]{1,0:T(8,128)(2,1)}, bf16[256,2048]{1,0:T(8,128)(2,1)S(1)}, u32[]{:S(2)}) copy-start(bf16[256,2048]{1,0:T(8,128)(2,1)S(1)} %get-tuple-element.26.dattn) | copy-start | bytes 3145732
  201.8 1.4 copy-start.21
  234.6 29.7 %all-to-all-start.6 = ((bf16[16,16,2048]{2,1,0:T(8,128)(2,1)}), bf16[16,16,2048]{2,1,0:T(8,128)(2,1)S(1)}, u32[]{:S(2)}, u32[]{:S(2)}) async-start(bf16[16,16,2048]{2,1,0:T(8,128)(2,1)} %bitcast.8), calls=%async_computation.6 | async-start | bytes 2097152 | tf_op jit(solution)/shard_map/all_to_all | solution.py:140
  264.3 1.0 copy-start.25
  265.3 29.0 %all-to-all-start.5 = ((bf16[16,16,2048]{2,1,0:T(8,128)(2,1)}), bf16[16,16,2048]{2,1,0:T(8,128)(2,1)}, u32[]{:S(2)}, u32[]{:S(2)}) async-start(bf16[16,16,2048]{2,1,0:T(8,128)(2,1)} %gather_fusion.2), calls=%async_computation.5 | async-start | bytes 2097152 | tf_op jit(solution)/shard_map/all_to_all | solution.py:140
  271.1 29.1 %copy-start.4 = (bf16[256,2048]{1,0:T(8,128)(2,1)S(1)}, bf16[256,2048]{1,0:T(8,128)(2,1)}, u32[]{:S(2)}) copy-start(bf16[256,2048]{1,0:T(8,128)(2,1)} %copy-done.1) | copy-start | bytes 3145732
  271.1 29.1 %copy-start.6 = (bf16[256,2048]{1,0:T(8,128)(2,1)S(1)}, bf16[256,2048]{1,0:T(8,128)(2,1)}, u32[]{:S(2)}) copy-start(bf16[256,2048]{1,0:T(8,128)(2,1)} %copy-done.5) | copy-start | bytes 3145732
  294.3 73.7 %all-to-all-start.7 = ((bf16[16,16,2048]{2,1,0:T(8,128)(2,1)}), bf16[16,16,2048]{2,1,0:T(8,128)(2,1)}, u32[]{:S(2)}, u32[]{:S(2)}) async-start(bf16[16,16,2048]{2,1,0:T(8,128)(2,1)} %gather_fusion.3), calls=%async_computation.7 | async-start | bytes 2097152 | tf_op jit(solution)/shard_map/all_to_all | solution.py:140
  300.2 1.6 copy-start.20
  301.8 1.6 copy-start.22
  303.4 13.1 %copy-start.9 = (bf16[256,2048]{1,0:T(8,128)(2,1)S(1)}, bf16[256,2048]{1,0:T(8,128)(2,1)}, u32[]{:S(2)}) copy-start(bf16[256,2048]{1,0:T(8,128)(2,1)} %ko.3) | copy-start | bytes 3145732
  303.4 13.1 %copy-start.18 = (bf16[16,256,256]{2,1,0:T(8,128)(2,1)S(1)}, bf16[16,256,256]{2,1,0:T(8,128)(2,1)}, u32[]{:S(2)}) copy-start(bf16[16,256,256]{2,1,0:T(8,128)(2,1)} %copy-done.17) | copy-start | bytes 6291460
  310.6 35.9 %collective-permute-start.2 = (bf16[256,2048]{1,0:T(8,128)(2,1)S(1)}, bf16[256,2048]{1,0:T(8,128)(2,1)S(1)}, u32[]{:S(2)}, u32[]{:S(2)}) collective-permute-start(bf16[256,2048]{1,0:T(8,128)(2,1)S(1)} %get-tuple-element.33), channel_id=1, source_target_pairs={{2,0},{4,2},{6,4},{8,6},{10,8},{12,10},{14,12},{16,14},{18,16},{20... | collective-permute-start | bytes 3145736 | tf_op jit(solution)/shard_map/ppermute | solution.py:136
  313.1 54.9 %collective-permute-start.3 = (bf16[256,2048]{1,0:T(8,128)(2,1)S(1)}, bf16[256,2048]{1,0:T(8,128)(2,1)}, u32[]{:S(2)}, u32[]{:S(2)}) collective-permute-start(bf16[256,2048]{1,0:T(8,128)(2,1)S(1)} %get-tuple-element.36), channel_id=1, source_target_pairs={{2,0},{4,2},{6,4},{8,6},{10,8},{12,10},{14,12},{16,14},{18,16},{20... | collective-permute-start | bytes 3145736 | tf_op jit(solution)/shard_map/ppermute | solution.py:136
  324.4 24.8 %copy-start.23 = (bf16[256,2048]{1,0:T(8,128)(2,1)}, bf16[256,2048]{1,0:T(8,128)(2,1)S(1)}, u32[]{:S(2)}) copy-start(bf16[256,2048]{1,0:T(8,128)(2,1)S(1)} %get-tuple-element.35) | copy-start | bytes 3145732

commit v2 on v1

v2 whole, which is shorter than its diff:
```python
import functools
import math

import jax
import jax.numpy as jnp
from jax import lax
from jax.experimental import pallas as pl
from jax.experimental.pallas import tpu as pltpu
from jax.sharding import PartitionSpec as P

HEADS = 32
HD = 128
BLOCK = 256
EPSILON = 1e-05
FACTOR = 1.0 / math.sqrt(HD)
LOG2E = math.log2(math.e)
MASKED = -1e30
F32 = jnp.float32
BF16 = jnp.bfloat16


def dot(a, b, contract):
    return lax.dot_general(a, b, (contract, ((), ())), preferred_element_type=F32)


NT = ((1,), (1,))
NN = ((1,), (0,))
TN = ((0,), (0,))


def head(h):
    return pl.ds(h * HD, HD)


def joined(parts, h):
    return jnp.concatenate([part[:, head(h)] for part in parts], axis=0)


def scores_kernel(group, index_ref, q, ko, kt, vo, *rest):
    kp = rest[:-4]
    pp_out, po_out, pt_out, acc_out = rest[-4:]
    first = index_ref[0] == 0
    rows = lax.broadcasted_iota(jnp.int32, (BLOCK, BLOCK), 0)
    cols = lax.broadcasted_iota(jnp.int32, (BLOCK, BLOCK), 1)
    causal = rows >= cols
    for h in range(group):
        here = q[:, head(h)]
        scale = FACTOR * LOG2E
        sp = jnp.where(first, MASKED, dot(here, joined(kp, h), NT) * scale)
        so = jnp.where(causal, dot(here, ko[:, head(h)], NT) * scale, MASKED)
        st = dot(here, kt[:, head(h)], NT) * scale
        top = jnp.max(jnp.maximum(jnp.maximum(sp, so), st), axis=1, keepdims=True)
        ep = jnp.exp2(sp - top)
        eo = jnp.exp2(so - top)
        et = jnp.exp2(st - top)
        inverse = 1.0 / jnp.sum(ep + eo + et, axis=1, keepdims=True)
        wo = (eo * inverse).astype(BF16)
        pp_out[h] = (ep * inverse).astype(BF16)
        po_out[h] = wo
        pt_out[h] = (et * inverse).astype(BF16)
        acc_out[:, head(h)] = dot(wo, vo[:, head(h)], NN)


def attn_kernel(group, steps, pp, pt, vt, acc, cot, gain, *rest):
    vp = rest[:-4]
    attn_out, sums_out, square, product = rest[-4:]
    step = pl.program_id(0)

    @pl.when(step == 0)
    def _():
        square[...] = jnp.zeros_like(square)
        product[...] = jnp.zeros_like(product)

    sq = square[...]
    pr = product[...]
    for h in range(group):
        total = acc[:, head(h)] + dot(pp[h], joined(vp, h), NN)
        low = (total + dot(pt[h], vt[:, head(h)], NN)).astype(BF16)
        attn_out[:, head(h)] = low
        wide = low.astype(F32)
        sq = sq + wide * wide
        pr = pr + gain[:, head(h)] * cot[:, head(h)].astype(F32) * wide
    square[...] = sq
    product[...] = pr

    @pl.when(step == steps - 1)
    def _():
        sums_out[0:1, :] = jnp.sum(jnp.transpose(square[...]), axis=0, keepdims=True)
        sums_out[1:2, :] = jnp.sum(jnp.transpose(product[...]), axis=0, keepdims=True)


def norm_terms(sums, features):
    table = jnp.concatenate([sums[...], jnp.zeros((6, BLOCK), F32)], axis=0)
    columns = jnp.transpose(table)
    rms = lax.rsqrt(columns[:, 0:1] / features + EPSILON)
    return rms, columns[:, 1:2] / features


def dattn_kernel(group, features, sums, attn, cot, gain, pt, dattn_out, dvt_out):
    rms, mean = norm_terms(sums, features)
    back = rms * rms * rms * mean
    for h in range(group):
        grad_in = gain[:, head(h)] * cot[:, head(h)].astype(F32)
        low = (rms * grad_in - attn[:, head(h)].astype(F32) * back).astype(BF16)
        dattn_out[:, head(h)] = low
        dvt_out[:, head(h)] = dot(pt[h], low, TN).astype(BF16)


def dscore_of(weights, dattn, attn, values):
    delta = jnp.sum(dattn.astype(F32) * attn.astype(F32), axis=1, keepdims=True)
    return (weights.astype(F32) * (dot(dattn, values, NT) - delta)).astype(BF16)


def partner_kernel(group, pt, dattn, attn, vt, kt, q, dq_in, dkt_out, dq_out):
    for h in range(group):
        ds = dscore_of(pt[h], dattn[:, head(h)], attn[:, head(h)], vt[:, head(h)])
        dkt_out[:, head(h)] = (dot(ds, q[:, head(h)], TN) * FACTOR).astype(BF16)
        dq_out[:, head(h)] = dq_in[:, head(h)] + dot(ds, kt[:, head(h)], NN)


def prior_kernel(group, pp, dattn, attn, q, *rest):
    dvp_out, dkp_out, dq_out = rest[-3:]
    vp, kp = rest[:2], rest[2:4]
    for h in range(group):
        low = dattn[:, head(h)]
        ds = dscore_of(pp[h], low, attn[:, head(h)], joined(vp, h))
        dvp_out[:, head(h)] = dot(pp[h], low, TN).astype(BF16)
        dkp_out[:, head(h)] = (dot(ds, q[:, head(h)], TN) * FACTOR).astype(BF16)
        dq_out[:, head(h)] = dot(ds, joined(kp, h), NN)


def finish_kernel(own, home, near_upper, near_lower, out):
    near = jnp.concatenate([near_upper[...], near_lower[...]], axis=0).astype(F32)
    out[...] = (own[...].astype(F32) + near + home[...].astype(F32)).astype(BF16)


def own_kernel(group, features, sums, po, dattn, attn, vo, ko, q, dq_in, gain, dvo_out, dko_out, dq_out, mixed_out):
    rms, _ = norm_terms(sums, features)
    for h in range(group):
        low = dattn[:, head(h)]
        ds = dscore_of(po[h], low, attn[:, head(h)], vo[:, head(h)])
        dvo_out[:, head(h)] = dot(po[h], low, TN).astype(BF16)
        dko_out[:, head(h)] = (dot(ds, q[:, head(h)], TN) * FACTOR).astype(BF16)
        dq_out[:, head(h)] = ((dq_in[:, head(h)] + dot(ds, ko[:, head(h)], NN)) * FACTOR).astype(BF16)
        mixed_out[:, head(h)] = (attn[:, head(h)].astype(F32) * rms * gain[:, head(h)]).astype(BF16)


def shift(value, steps):
    count = lax.axis_size("ctx")
    first, last = (max(0, -steps), min(count, count - steps))
    return lax.ppermute(value, "ctx", [(source, source + steps) for source in range(first, last)])


def upper(value):
    return value[: value.shape[0] // 2]


def lower(value):
    return value[value.shape[0] // 2 :]


def half_exchange(pieces):
    count = lax.axis_size("ctx")
    half = count // 2
    groups = [list(range(half)), list(range(half, count))]
    return lax.all_to_all(
        pieces, "ctx", split_axis=0, concat_axis=0, tiled=True, axis_index_groups=groups
    )


def spread(value):
    half = lax.axis_size("ctx") // 2
    return half_exchange(value.reshape(half, value.shape[0] // half, value.shape[1]))


def collect(pieces):
    return half_exchange(pieces).reshape(pieces.shape[0] * pieces.shape[1], pieces.shape[2])


def plan_kernel(count, unit, index, pairing, *refs):
    half = count // 2
    inverse, rank = refs[-2:]
    base = jnp.where(index[0] >= half, half, 0)

    def invert(block, carry):
        inverse[pairing[block]] = block
        return carry

    lax.fori_loop(0, count, invert, 0)
    for way, (wanted, holders) in enumerate(((pairing, inverse), (inverse, pairing))):
        level, order, pick = refs[3 * way : 3 * way + 3]

        def clear(slot, carry):
            order[slot] = 0
            return carry

        def number(block, total):
            leaves = (holders[block] >= half) != (block >= half)
            rank[block] = total

            @pl.when(leaves & (block >= base) & (block < base + half))
            def _():
                order[total] = block - base

            return total + leaves.astype(jnp.int32)

        def place(slot, carry):
            source = wanted[base + slot]
            inside = (source >= base) & (source < base + half)
            pick[slot] = jnp.where(inside, source - base, half + rank[source])
            return carry

        lax.fori_loop(0, half, clear, 0)
        total = lax.fori_loop(0, half, number, jnp.int32(0))
        lax.fori_loop(half, count, number, jnp.int32(0))
        lax.fori_loop(0, half, place, 0)
        level[0] = (total + unit - 1) // unit


def make_plans(index, pairing):
    count = pairing.shape[0]
    half = count // 2
    smem = pl.BlockSpec(memory_space=pltpu.SMEM)
    shapes = [jax.ShapeDtypeStruct((size,), jnp.int32) for size in (1, half, half)]
    plans = pl.pallas_call(
        functools.partial(plan_kernel, count, -(-half // 8)),
        name="plan",
        in_specs=[smem, smem],
        out_specs=[smem] * 6,
        out_shape=shapes * 2,
        scratch_shapes=[pltpu.SMEM((count,), jnp.int32)] * 2,
    )(index, pairing)
    return plans[:3], plans[3:]


def pick_kernel(half, pick, pieces, *rest):
    out, sems = rest[-2:]
    size = out.shape[0]
    for t in range(size):
        index = pick[t]
        if len(rest) == 2:
            pltpu.make_async_copy(pieces.at[index], out.at[t], sems.at[t]).start()
            continue

        @pl.when(index < half)
        def _():
            pltpu.make_async_copy(pieces.at[index], out.at[t], sems.at[t]).start()

        @pl.when(index >= half)
        def _():
            pltpu.make_async_copy(rest[0].at[index - half], out.at[t], sems.at[t]).start()

    for t in range(size):
        pltpu.make_async_copy(pieces.at[0], out.at[t], sems.at[t]).wait()


def pick_pieces(pick, size, *sources):
    half = sources[0].shape[0]
    shape = (size,) + sources[0].shape[1:]
    return pl.pallas_call(
        functools.partial(pick_kernel, half),
        name="pick",
        in_specs=[pl.BlockSpec(memory_space=pltpu.SMEM)]
        + [pl.BlockSpec(memory_space=pl.ANY)] * len(sources),
        out_specs=pl.BlockSpec(memory_space=pltpu.VMEM),
        out_shape=jax.ShapeDtypeStruct(shape, sources[0].dtype),
        scratch_shapes=[pltpu.SemaphoreType.DMA((size,))],
        cost_estimate=pl.CostEstimate(
            flops=0, bytes_accessed=4 * math.prod(shape), transcendentals=0
        ),
    )(pick, *sources)


def cross(pieces, plan, beside, extras):
    level, order, pick = plan
    count = lax.axis_size("ctx")
    half = count // 2
    unit = -(-half // 8)
    pairs = [(i, (i + half) % count) for i in range(count)]

    def branch(number):
        size = min(number * unit, half)

        def run(pieces, order, pick, *extras):
            sources = [pieces]
            if size:
                leaving = pick_pieces(order, size, pieces)
                leaving, *extras = lax.optimization_barrier((leaving, *extras))
                sources.append(lax.ppermute(leaving, "ctx", pairs))
            moved = beside(*extras)
            return pick_pieces(pick, half, *sources), moved

        return run

    levels = -(-half // unit) + 1
    return lax.switch(
        level[0],
        [branch(number) for number in range(levels)],
        pieces,
        order,
        pick,
        *extras,
    )


def stage(pairing, body, *args):
    shapes = jax.eval_shape(body, *args)

    def empty(*args):
        return jax.tree.map(lambda leaf: jnp.zeros(leaf.shape, leaf.dtype), shapes)

    return lax.cond(pairing[0] >= 0, body, empty, *args)


def on_device(queries, key_rows, value_rows, cotangent, norm_gain, pairing):
    width = queries.shape[1]
    heads = width // HD
    group = math.gcd(4, heads)
    steps = heads // group
    features = float(HEADS * HD)
    wide = pl.BlockSpec((BLOCK, group * HD), lambda g: (0, g))
    square = pl.BlockSpec((group, BLOCK, BLOCK), lambda g: (g, 0, 0))
    line = pl.BlockSpec((1, group * HD), lambda g: (0, g))
    whole = pl.BlockSpec((2, BLOCK), lambda g: (0, 0))
    rows_low = jax.ShapeDtypeStruct((BLOCK, width), BF16)
    rows_wide = jax.ShapeDtypeStruct((BLOCK, width), F32)
    weights = jax.ShapeDtypeStruct((heads, BLOCK, BLOCK), BF16)

    def call(body, name, ins, outs, shapes, dots, exps=0, scratch=()):
        return pl.pallas_call(
            body,
            name=name,
            grid=(steps,),
            in_specs=ins,
            out_specs=outs,
            out_shape=shapes,
            scratch_shapes=scratch,
            compiler_params=pltpu.CompilerParams(vmem_limit_bytes=56 * 2**20),
            cost_estimate=pl.CostEstimate(
                flops=dots * heads * 2 * BLOCK * BLOCK * HD,
                bytes_accessed=(len(ins) + 2) * BLOCK * width * 2,
                transcendentals=exps * heads * BLOCK * BLOCK,
            ),
        )

    gain = norm_gain.reshape(1, width)
    index = lax.axis_index("ctx").astype(jnp.int32).reshape(1)
    part = pl.BlockSpec((BLOCK // 2, group * HD), lambda g: (0, g))
    smem = pl.BlockSpec(memory_space=pltpu.SMEM)

    def first_stage(keys, index, pairing):
        return spread(keys), shift(upper(keys), 1), make_plans(index, pairing)

    keys_spread, kp_upper, (plan, plan_back) = stage(
        pairing, first_stage, key_rows, index, pairing
    )
    keys_crossed, (kp_lower, values_spread) = cross(
        keys_spread,
        plan,
        lambda keys, values: (shift(lower(keys), 1), spread(values)),
        (key_rows, value_rows),
    )
    values_crossed, (vp_upper, kt) = cross(
        values_spread,
        plan,
        lambda values, crossed: (shift(upper(values), 1), collect(crossed)),
        (value_rows, keys_crossed),
    )

    def last_stage(crossed, index, q, ko, kt, vo, kp_upper, kp_lower):
        weighed = call(
            functools.partial(scores_kernel, group),
            "scores",
            [smem] + [wide] * 4 + [part] * 2,
            [square] * 3 + [wide],
            [weights] * 3 + [rows_wide],
            4,
            3,
        )(index, q, ko, kt, vo, kp_upper, kp_lower)
        return weighed, collect(crossed), shift(lower(vo), 1)

    (pp, po, pt, acc), vt, vp_lower = stage(
        pairing,
        last_stage,
        values_crossed,
        index,
        queries,
        key_rows,
        kt,
        value_rows,
        kp_upper,
        kp_lower,
    )
    attn, sums = call(
        functools.partial(attn_kernel, group, steps),
        "attn",
        [square, square, wide, wide, wide, line] + [part] * 2,
        [wide, whole],
        [rows_low, jax.ShapeDtypeStruct((2, BLOCK), F32)],
        2,
        scratch=[pltpu.VMEM((BLOCK, HD), F32)] * 2,
    )(pp, pt, vt, acc, cotangent, gain, vp_upper, vp_lower)
    sums = lax.psum(sums, "head")
    dattn, dvt = call(
        functools.partial(dattn_kernel, group, features),
        "dattn",
        [whole, wide, wide, line, square],
        [wide, wide],
        [rows_low] * 2,
        1,
    )(sums, attn, cotangent, gain, pt)

    def first_back(dvt, pp, pt, dattn, attn, vt, kt, q, *near):
        dvp, dkp, dq = call(
            functools.partial(prior_kernel, group),
            "prior",
            [square] + [wide] * 3 + [part] * 4,
            [wide] * 3,
            [rows_low, rows_low, rows_wide],
            4,
        )(pp, dattn, attn, q, *near)
        dkt, dq = call(
            functools.partial(partner_kernel, group),
            "partner",
            [square] + [wide] * 6,
            [wide, wide],
            [rows_low, rows_wide],
            3,
        )(pt, dattn, attn, vt, kt, q, dq)
        return spread(dvt), dvp, dkp, dkt, dq, shift(upper(dvp), -1)

    dvt_spread, dvp, dkp, dkt, dq, dvn_upper = stage(
        pairing,
        first_back,
        dvt,
        pp,
        pt,
        dattn,
        attn,
        vt,
        kt,
        queries,
        vp_upper,
        vp_lower,
        kp_upper,
        kp_lower,
    )
    dvt_crossed, (dvn_lower, dkt_spread) = cross(
        dvt_spread,
        plan_back,
        lambda values, keys: (shift(lower(values), -1), spread(keys)),
        (dvp, dkt),
    )
    dkt_crossed, (dkn_upper, dvt_home) = cross(
        dkt_spread,
        plan_back,
        lambda keys, crossed: (shift(upper(keys), -1), collect(crossed)),
        (dkp, dvt_crossed),
    )

    def finish(*terms):
        return call(finish_kernel, "finish", [wide] * 2 + [part] * 2, wide, rows_low, 0)(*terms)

    def last_back(crossed, sums, po, dattn, attn, vo, ko, q, dq, gain, dkp, *terms):
        dvo, dko, grad_query, mixed = call(
            functools.partial(own_kernel, group, features),
            "own",
            [whole, square] + [wide] * 6 + [line],
            [wide] * 4,
            [rows_low] * 4,
            4,
        )(sums, po, dattn, attn, vo, ko, q, dq, gain)
        grad_value = finish(dvo, *terms)
        return mixed, grad_query, grad_value, dko, collect(crossed), shift(lower(dkp), -1)

    mixed, grad_query, grad_value, dko, dkt_home, dkn_lower = stage(
        pairing,
        last_back,
        dkt_crossed,
        sums,
        po,
        dattn,
        attn,
        value_rows,
        key_rows,
        queries,
        dq,
        gain,
        dkp,
        dvt_home,
        dvn_upper,
        dvn_lower,
    )
    grad_key = finish(dko, dkt_home, dkn_upper, dkn_lower)
    return mixed, grad_query, grad_key, grad_value


def solution(mesh):
    rows = P("ctx", "head")
    return jax.shard_map(
        on_device,
        mesh=mesh,
        in_specs=(rows, rows, rows, rows, P("head"), P()),
        out_specs=(rows, rows, rows, rows),
        check_vma=False,
    )
```

time: 373 us -> 337 us (0.903)
  blocking collectives: 65.3 us -> 2.58 us
  Pallas kernels: 38.3 us -> 76.5 us
  starting transfers between devices: 48.2 us -> 74.8 us
  local copies, waits for them, and re-layouts: 28.4 us -> 6.5 us
  waiting for transfers between devices: 184 us -> 169 us
  other arithmetic: 6.32 us -> 0 us
    all_to_all x6 -> x8, waiting for transfers between devices: 84.3 us -> 0.86 us  [half_exchange(): lax.all_to_all(pieces, 'ctx', split_axis=0, concat_axis=0, tiled=True, ax...]
    ppermute x4 -> x12, waiting for transfers between devices: 99.9 us -> 168 us  [the longest x4 99.1 us: run(): sources.append(lax.ppermute(leaving, 'ctx', pairs))]
    all_to_all x2 -> x0, blocking collectives: 62.8 us -> none  [exchange(): lax.all_to_all(pieces, 'ctx', split_axis=0, concat_axis=0, tiled=True)]
    pallas_call x5 -> x16, Pallas kernels: 34.7 us -> 71.4 us  [the longest x8 22 us: pick_pieces(): pl.pallas_call(functools.partial(pick_kernel, half), name='pick', in_spec...]
    ppermute x4 -> x12, starting transfers between devices: 12.6 us -> 33.2 us  [the longest x8 22.1 us: shift(): lax.ppermute(value, 'ctx', [(source, source + steps) for source in range(...]
    unnamed x56 -> x12, local copies, waits for them, and re-layouts: 19.3 us -> 0.03 us
    gather x4 -> x0, local copies, waits for them, and re-layouts: 9.08 us -> none  [collect(): chosen = jnp.take(pieces, wanted, axis=0, mode='clip')]
    convert_element_type x2 -> x0, other arithmetic: 6.19 us -> none  [the longest x1 3.41 us: on_device(): (dvo.astype(F32) + dvn.astype(F32) + dvt_home.astype(F32)).astype(BF16)]
  transfers between devices with their start and end apart: 10 -> 20, of which waited for: 8 -> 13; matrix products, arithmetic and copies ran while one was open for 3% -> 2% of each run, Pallas kernels for 7% -> 15%
where the time goes in v2:
time: 337 us; the launch traced here: 332 us
  waiting for transfers between devices  169 us (50%)
  Pallas kernels  76.5 us (23%)
  starting transfers between devices  74.8 us (22%)
  local copies, waits for them, and re-layouts  6.5 us (2%)
    ppermute x4, waiting for transfers between devices, run(): sources.append(lax.ppermute(leaving, 'ctx', pairs))  99.1 us
    ppermute x8, waiting for transfers between devices, shift(): lax.ppermute(value, 'ctx', [(source, source + steps) for source in range(...  69.1 us
    all_to_all x8, starting transfers between devices, half_exchange(): lax.all_to_all(pieces, 'ctx', split_axis=0, concat_axis=0, tiled=True, ax...  41.6 us
    ppermute x8, starting transfers between devices, shift(): lax.ppermute(value, 'ctx', [(source, source + steps) for source in range(...  22.1 us
    pallas_call x8, Pallas kernels, pick_pieces(): pl.pallas_call(functools.partial(pick_kernel, half), name='pick', in_spec...  22 us
    ppermute x4, starting transfers between devices, run(): sources.append(lax.ppermute(leaving, 'ctx', pairs))  11.2 us
    pallas_call x1, Pallas kernels, last_stage(): call(functools.partial(scores_kernel, group), 'scores', [smem] + [wide] *...  10.4 us
    pallas_call x1, Pallas kernels, last_back(): call(functools.partial(own_kernel, group, features), 'own', [whole, squar...  8.49 us
  transfers between devices with their start and end apart: 20, of which 13 were waited for; matrix products, arithmetic and copies ran while one was open for 2% of the time, Pallas kernels for 15%

profile of v2, /device:TPU:14, one launch (start us, length us, event | category | flops | bytes accessed | tf_op | source)
XLA Modules:
  0.0 332.5 jit_solution(2645018527376655661)
XLA Ops:
  1.3 30.8 %conditional.8 = (bf16[8,32,2048]{2,1,0:T(8,128)(2,1)}, bf16[128,2048]{1,0:T(8,128)(2,1)}, s32[1]{0:T(128)}, s32[8]{0:T(128)S(1)}, s32[8]{0:T(128)S(1)}, /*index=5*/s32[1]{0:T(128)}, s32[8]{0:T(128)S(1)}, s32[8]{0:T(128)S(1)}) conditional(s32[]{:T(128)} %bitcast.40, () %tuple.218, (bf16[256,2048]{1,0:T(8,128)(2,1)}, s32[1]{0:T(128)}, ...), branch_computations={%region_0.0_spmd, %region_1.0_spmd} | conditional | bytes 10486208 | solution.py:312
  1.3 5.2 %all-to-all-start = ((bf16[8,32,2048]{2,1,0:T(8,128)(2,1)}), bf16[8,32,2048]{2,1,0:T(8,128)(2,1)}, u32[]{:S(2)}, u32[]{:S(2)}) async-start(bf16[8,32,2048]{2,1,0:T(8,128)(2,1)} %bitcast.55), calls=%async_computation | async-start | bytes 2097152 | tf_op jit(solution)/shard_map/cond/branch_1_fun/all_to_all | solution.py:166
  6.6 3.0 collective-permute-start
  11.6 19.2 %collective-permute-done = bf16[128,2048]{1,0:T(8,128)(2,1)} collective-permute-done((bf16[128,2048]{1,0:T(8,128)(2,1)S(1)}, bf16[128,2048]{1,0:T(8,128)(2,1)}, u32[]{:S(2)}, u32[]{:S(2)}) %collective-permute-start) | collective-permute-done | bytes 524320 | tf_op jit(solution)/shard_map/cond/branch_1_fun/ppermute | solution.py:151
  32.1 49.6 %conditional.9 = (bf16[8,32,2048]{2,1,0:T(8,128)(2,1)}, bf16[128,2048]{1,0:T(8,128)(2,1)}, bf16[8,32,2048]{2,1,0:T(8,128)(2,1)}) conditional(s32[]{:T(128)} %bitcast.42, (s32[8]{0:T(128)S(1)}, bf16[8,32,2048]{2,1,0:T(8,128)(2,1)}, bf16[256,2048]{1,0:T(8,128)(2,1)}, bf16[256,2048]{1,0:T(8,128)(2,1)S(1)}) %tuple.277, ...), branch_computations={%region_2.0_spmd, %region_3.0_spmd, %region_4.0_spmd, %region_5.0_... | conditional | bytes 27263196 | solution.py:296
  32.1 2.6 pick.77
  34.7 5.2 %all-to-all-start.6 = ((bf16[8,32,2048]{2,1,0:T(8,128)(2,1)S(1)}), bf16[8,32,2048]{2,1,0:T(8,128)(2,1)}, u32[]{:S(2)}, u32[]{:S(2)}) async-start(bf16[8,32,2048]{2,1,0:T(8,128)(2,1)S(1)} %bitcast.51), calls=%async_computation.6 | async-start | bytes 2097152 | tf_op jit(solution)/shard_map/cond/branch_5_fun/all_to_all | solution.py:166
  40.0 2.6 collective-permute-start.10
  45.4 26.5 %collective-permute-done.10.rest_0_ = bf16[5,32,2048]{2,1,0:T(8,128)(2,1)S(1)} collective-permute-done((bf16[5,32,2048]{2,1,0:T(8,128)(2,1)S(1)}, bf16[5,32,2048]{2,1,0:T(8,128)(2,1)S(1)}, u32[]{:S(2)}, u32[]{:S(2)}) %collective-permute-start.10) | collective-permute-done | bytes 655392 | tf_op jit(solution)/shard_map/cond/branch_5_fun/ppermute | solution.py:289
  72.7 2.9 pick.78
  75.6 6.1 %collective-permute-done.11 = bf16[128,2048]{1,0:T(8,128)(2,1)} collective-permute-done((bf16[128,2048]{1,0:T(8,128)(2,1)}, bf16[128,2048]{1,0:T(8,128)(2,1)}, u32[]{:S(2)}, u32[]{:S(2)}) %collective-permute-start.11) | collective-permute-done | bytes 524320 | tf_op jit(solution)/shard_map/cond/branch_5_fun/ppermute | solution.py:151
  81.7 50.7 %conditional.10 = (bf16[8,32,2048]{2,1,0:T(8,128)(2,1)}, bf16[128,2048]{1,0:T(8,128)(2,1)}, bf16[256,2048]{1,0:T(8,128)(2,1)}) conditional(s32[]{:T(128)} %bitcast.42, (s32[8]{0:T(128)S(1)}, bf16[8,32,2048]{2,1,0:T(8,128)(2,1)}, bf16[256,2048]{1,0:T(8,128)(2,1)S(1)}, bf16[8,32,2048]{2,1,0:T(8,128)(2,1)}) %tuple.286, ...), branch_computations={%region_11.0_spmd, %region_12.0_spmd, %region_13.0_spmd, %region_1... | conditional | bytes 14680200 | solution.py:296
  81.7 2.7 pick.94
  84.3 5.1 %all-to-all-start.15 = ((bf16[8,32,2048]{2,1,0:T(8,128)(2,1)}), bf16[8,32,2048]{2,1,0:T(8,128)(2,1)}, u32[]{:S(2)}, u32[]{:S(2)}) async-start(bf16[8,32,2048]{2,1,0:T(8,128)(2,1)} %get-tuple-element.546), calls=%async_computation.15 | async-start | bytes 2097152 | tf_op jit(solution)/shard_map/cond/branch_5_fun/all_to_all | solution.py:166
  89.4 4.8 %collective-permute-start.27 = (bf16[5,32,2048]{2,1,0:T(8,128)(2,1)}, bf16[5,32,2048]{2,1,0:T(8,128)(2,1)}, u32[]{:S(2)}, u32[]{:S(2)}) collective-permute-start(bf16[5,32,2048]{2,1,0:T(8,128)(2,1)} %pick.94), channel_id=1, source_target_pairs={{0,16},{2,18},{4,20},{6,22},{8,24},{10,26},{12,28},{14,30},{16,0},... | collective-permute-start | bytes 1966088 | tf_op jit(solution)/shard_map/cond/branch_5_fun/ppermute | solution.py:289
  97.0 26.8 %collective-permute-done.27.rest_0_ = bf16[5,32,2048]{2,1,0:T(8,128)(2,1)} collective-permute-done((bf16[5,32,2048]{2,1,0:T(8,128)(2,1)}, bf16[5,32,2048]{2,1,0:T(8,128)(2,1)}, u32[]{:S(2)}, u32[]{:S(2)}) %collective-permute-start.27) | collective-permute-done | bytes 655392 | tf_op jit(solution)/shard_map/cond/branch_5_fun/ppermute | solution.py:289
  123.8 2.9 pick.95
  126.7 5.6 %collective-permute-done.28 = bf16[128,2048]{1,0:T(8,128)(2,1)} collective-permute-done((bf16[128,2048]{1,0:T(8,128)(2,1)}, bf16[128,2048]{1,0:T(8,128)(2,1)}, u32[]{:S(2)}, u32[]{:S(2)}) %collective-permute-start.28) | collective-permute-done | bytes 524320 | tf_op jit(solution)/shard_map/cond/branch_5_fun/ppermute | solution.py:151
  132.4 26.4 %conditional.11 = (bf16[16,256,256]{2,1,0:T(8,128)(2,1)}, bf16[16,256,256]{2,1,0:T(8,128)(2,1)}, bf16[16,256,256]{2,1,0:T(8,128)(2,1)}, f32[256,2048]{1,0:T(8,12...) conditional(s32[]{:T(128)} %bitcast.40, () %tuple.217, (s32[1]{0:T(128)}, ...), branch_computations={%region_20.0_spmd, %region_21.0_spmd} | conditional | flops 1073741824 | bytes 15728760 | solution.py:312
  132.4 5.1 %all-to-all-start.19 = ((bf16[8,32,2048]{2,1,0:T(8,128)(2,1)}), bf16[8,32,2048]{2,1,0:T(8,128)(2,1)}, u32[]{:S(2)}, u32[]{:S(2)}) async-start(bf16[8,32,2048]{2,1,0:T(8,128)(2,1)} %get-tuple-element.582), calls=%async_computation.19 | async-start | bytes 2097152 | tf_op jit(solution)/shard_map/cond/branch_1_fun/all_to_all | solution.py:166
  137.6 5.3 %collective-permute-start.35 = (bf16[128,2048]{1,0:T(8,128)(2,1)S(1)}, bf16[128,2048]{1,0:T(8,128)(2,1)}, u32[]{:S(2)}, u32[]{:S(2)}) collective-permute-start(bf16[128,2048]{1,0:T(8,128)(2,1)S(1)} %slice.104), channel_id=1, source_target_pairs={{0,2},{2,4},{4,6},{6,8},{8,10},{10,12},{12,14},{14,16},{16,18},{18... | collective-permute-start | bytes 1572872 | tf_op jit(solution)/shard_map/cond/branch_1_fun/ppermute | solution.py:151
  142.9 10.4 %scores.1 = (bf16[16,256,256]{2,1,0:T(8,128)(2,1)}, bf16[16,256,256]{2,1,0:T(8,128)(2,1)}, bf16[16,256,256]{2,1,0:T(8,128)(2,1)}, f32[256,2048]{1,0:T(8,128)}) custom-call(s32[1]{0:T(128)} %get-tuple-element.571.index_ref, bf16[256,2048]{1,0:T(8,128)(2,1)S(1)} %get-tuple-element.572.q, bf16[256,2048]{1,0:T(8,128)(2,1)S(1)} %get-tuple-element.573.ko, ...), custom_call_target="tpu_custom_call" | custom-call | flops 1073741824 | bytes 9437184 | tf_op jit(solution)/shard_map/cond/branch_1_fun/scores/pallas_call | solution.py:371
  153.3 5.5 %collective-permute-done.35 = bf16[128,2048]{1,0:T(8,128)(2,1)} collective-permute-done((bf16[128,2048]{1,0:T(8,128)(2,1)S(1)}, bf16[128,2048]{1,0:T(8,128)(2,1)}, u32[]{:S(2)}, u32[]{:S(2)}) %collective-permute-start.35) | collective-permute-done | bytes 524320 | tf_op jit(solution)/shard_map/cond/branch_1_fun/ppermute | solution.py:151
  158.8 5.7 %attn.1 = (bf16[256,2048]{1,0:T(8,128)(2,1)S(1)}, f32[2,256]{1,0:T(2,128)}) custom-call(bf16[16,256,256]{2,1,0:T(8,128)(2,1)} %get-tuple-element.810.pp, bf16[16,256,256]{2,1,0:T(8,128)(2,1)} %get-tuple-element.811.pt, bf16[256,2048]{1,0:T(8,128)(2,1)} %get-tuple-element.812.vt, f32[256,2048]{1,0:T(8,128)} %get-tuple-element.813.acc, bf16[256,2048]{1,0:T(8,128)(2,1)} %cot.3, ...), custom_call_target="tpu_custom_call" | custom-call | flops 536870912 | bytes 10485760 | tf_op jit(solution)/shard_map/attn/pallas_call | solution.py:394
  167.1 5.2 %dattn.1 = (bf16[256,2048]{1,0:T(8,128)(2,1)}, bf16[256,2048]{1,0:T(8,128)(2,1)}) custom-call(f32[2,256]{1,0:T(2,128)S(1)} %psum.7.sums, bf16[256,2048]{1,0:T(8,128)(2,1)S(1)} %get-tuple-element.818.attn, bf16[256,2048]{1,0:T(8,128)(2,1)} %cot.3, f32[1,2048]{1,0:T(1,128)S(1)} %bitcast.59, bf16[16,256,256]{2,1,0:T(8,128)(2,1)} %get-tuple-element.811.pt), custom_call_target="tpu_custom_call" | custom-call | flops 268435456 | bytes 7340032 | tf_op jit(solution)/shard_map/dattn/pallas_call | solution.py:404
  172.3 34.0 %conditional.12 = (bf16[8,32,2048]{2,1,0:T(8,128)(2,1)}, bf16[256,2048]{1,0:T(8,128)(2,1)}, bf16[256,2048]{1,0:T(8,128)(2,1)S(1)}, bf16[256,2048]{1,0:T(8,128)(2...) conditional(s32[]{:T(128)} %bitcast.40, () %tuple.225, (bf16[256,2048]{1,0:T(8,128)(2,1)}, ...), branch_computations={%region_23.0_spmd, %region_24.0_spmd} | conditional | flops 1879048192 | bytes 42991848 | solution.py:312
  172.3 5.4 %all-to-all-start.20 = ((bf16[8,32,2048]{2,1,0:T(8,128)(2,1)}), bf16[8,32,2048]{2,1,0:T(8,128)(2,1)}, u32[]{:S(2)}, u32[]{:S(2)}) async-start(bf16[8,32,2048]{2,1,0:T(8,128)(2,1)} %bitcast.56), calls=%async_computation.20 | async-start | bytes 2097152 | tf_op jit(solution)/shard_map/cond/branch_1_fun/all_to_all | solution.py:166
  177.7 8.2 %prior.1 = (bf16[256,2048]{1,0:T(8,128)(2,1)}, bf16[256,2048]{1,0:T(8,128)(2,1)S(1)}, f32[256,2048]{1,0:T(8,128)}) custom-call(bf16[16,256,256]{2,1,0:T(8,128)(2,1)} %get-tuple-element.584.pp, bf16[256,2048]{1,0:T(8,128)(2,1)} %get-tuple-element.585.dattn, bf16[256,2048]{1,0:T(8,128)(2,1)} %copy-done.13, bf16[256,2048]{1,0:T(8,128)(2,1)} %get-tuple-element.587.q, ...), custom_call_target="tpu_custom_call" | custom-call | flops 1073741824 | bytes 10485760 | tf_op jit(solution)/shard_map/cond/branch_1_fun/prior/pallas_call | solution.py:414
  189.5 7.7 %partner.1 = (bf16[256,2048]{1,0:T(8,128)(2,1)}, f32[256,2048]{1,0:T(8,128)}) custom-call(bf16[16,256,256]{2,1,0:T(8,128)(2,1)} %get-tuple-element.594.pt, bf16[256,2048]{1,0:T(8,128)(2,1)S(1)} %copy-done.17, bf16[256,2048]{1,0:T(8,128)(2,1)S(1)} %copy-done.14, bf16[256,2048]{1,0:T(8,128)(2,1)} %get-tuple-element.595.vt, ...), custom_call_target="tpu_custom_call" | custom-call | flops 805306368 | bytes 9437184 | tf_op jit(solution)/shard_map/cond/branch_1_fun/partner/pallas_call | solution.py:422
  197.3 9.0 %collective-permute-done.36 = bf16[128,2048]{1,0:T(8,128)(2,1)} collective-permute-done((bf16[128,2048]{1,0:T(8,128)(2,1)S(1)}, bf16[128,2048]{1,0:T(8,128)(2,1)}, u32[]{:S(2)}, u32[]{:S(2)}) %collective-permute-start.36) | collective-permute-done | bytes 524320 | tf_op jit(solution)/shard_map/cond/branch_1_fun/ppermute | solution.py:151
  206.3 49.2 %conditional.13 = (bf16[8,32,2048]{2,1,0:T(8,128)(2,1)}, bf16[128,2048]{1,0:T(8,128)(2,1)}, bf16[8,32,2048]{2,1,0:T(8,128)(2,1)}) conditional(s32[]{:T(128)} %bitcast.44, (s32[8]{0:T(128)S(1)}, bf16[8,32,2048]{2,1,0:T(8,128)(2,1)}, bf16[256,2048]{1,0:T(8,128)(2,1)}, bf16[256,2048]{1,0:T(8,128)(2,1)}) %tuple.227, ...), branch_computations={%region_25.0_spmd, %region_26.0_spmd, %region_27.0_spmd, %region_2... | conditional | bytes 14680200 | solution.py:296
  208.9 5.1 %all-to-all-start.26 = ((bf16[8,32,2048]{2,1,0:T(8,128)(2,1)}), bf16[8,32,2048]{2,1,0:T(8,128)(2,1)}, u32[]{:S(2)}, u32[]{:S(2)}) async-start(bf16[8,32,2048]{2,1,0:T(8,128)(2,1)} %bitcast.26), calls=%async_computation.26 | async-start | bytes 2097152 | tf_op jit(solution)/shard_map/cond/branch_5_fun/all_to_all | solution.py:166
  214.0 3.7 %collective-permute-start.46 = (bf16[5,32,2048]{2,1,0:T(8,128)(2,1)}, bf16[5,32,2048]{2,1,0:T(8,128)(2,1)}, u32[]{:S(2)}, u32[]{:S(2)}) collective-permute-start(bf16[5,32,2048]{2,1,0:T(8,128)(2,1)} %pick.111), channel_id=1, source_target_pairs={{0,16},{2,18},{4,20},{6,22},{8,24},{10,26},{12,28},{14,30},{16,0},... | collective-permute-start | bytes 1966088 | tf_op jit(solution)/shard_map/cond/branch_5_fun/ppermute | solution.py:289
  222.0 22.7 %collective-permute-done.46.rest_0_ = bf16[5,32,2048]{2,1,0:T(8,128)(2,1)} collective-permute-done((bf16[5,32,2048]{2,1,0:T(8,128)(2,1)}, bf16[5,32,2048]{2,1,0:T(8,128)(2,1)}, u32[]{:S(2)}, u32[]{:S(2)}) %collective-permute-start.46) | collective-permute-done | bytes 655392 | tf_op jit(solution)/shard_map/cond/branch_5_fun/ppermute | solution.py:289
  244.7 2.9 pick.112
  247.6 7.9 %collective-permute-done.47 = bf16[128,2048]{1,0:T(8,128)(2,1)} collective-permute-done((bf16[128,2048]{1,0:T(8,128)(2,1)}, bf16[128,2048]{1,0:T(8,128)(2,1)}, u32[]{:S(2)}, u32[]{:S(2)}) %collective-permute-start.47) | collective-permute-done | bytes 524320 | tf_op jit(solution)/shard_map/cond/branch_5_fun/ppermute | solution.py:151
  255.5 47.3 %conditional.14 = (bf16[8,32,2048]{2,1,0:T(8,128)(2,1)}, bf16[128,2048]{1,0:T(8,128)(2,1)}, bf16[256,2048]{1,0:T(8,128)(2,1)}) conditional(s32[]{:T(128)} %bitcast.44, (s32[8]{0:T(128)S(1)}, bf16[8,32,2048]{2,1,0:T(8,128)(2,1)}, bf16[256,2048]{1,0:T(8,128)(2,1)S(1)}, bf16[8,32,2048]{2,1,0:T(8,128)(2,1)}) %tuple.229, ...), branch_computations={%region_34.0_spmd, %region_35.0_spmd, %region_36.0_spmd, %region_3... | conditional | bytes 14680200 | solution.py:296
  255.5 2.6 pick.128
  258.1 5.1 %all-to-all-start.35 = ((bf16[8,32,2048]{2,1,0:T(8,128)(2,1)}), bf16[8,32,2048]{2,1,0:T(8,128)(2,1)}, u32[]{:S(2)}, u32[]{:S(2)}) async-start(bf16[8,32,2048]{2,1,0:T(8,128)(2,1)} %get-tuple-element.711), calls=%async_computation.35 | async-start | bytes 2097152 | tf_op jit(solution)/shard_map/cond/branch_5_fun/all_to_all | solution.py:166
  266.6 23.1 %collective-permute-done.63.rest_0_ = bf16[5,32,2048]{2,1,0:T(8,128)(2,1)} collective-permute-done((bf16[5,32,2048]{2,1,0:T(8,128)(2,1)}, bf16[5,32,2048]{2,1,0:T(8,128)(2,1)}, u32[]{:S(2)}, u32[]{:S(2)}) %collective-permute-start.63) | collective-permute-done | bytes 655392 | tf_op jit(solution)/shard_map/cond/branch_5_fun/ppermute | solution.py:289
  289.7 2.9 pick.129
  292.6 10.1 %collective-permute-done.64 = bf16[128,2048]{1,0:T(8,128)(2,1)} collective-permute-done((bf16[128,2048]{1,0:T(8,128)(2,1)}, bf16[128,2048]{1,0:T(8,128)(2,1)}, u32[]{:S(2)}, u32[]{:S(2)}) %collective-permute-start.64) | collective-permute-done | bytes 524320 | tf_op jit(solution)/shard_map/cond/branch_5_fun/ppermute | solution.py:151
  302.8 25.6 %conditional.15 = (bf16[256,2048]{1,0:T(8,128)(2,1)}, bf16[256,2048]{1,0:T(8,128)(2,1)}, bf16[256,2048]{1,0:T(8,128)(2,1)S(1)}, bf16[256,2048]{1,0:T(8,128)(2,1)...) conditional(s32[]{:T(128)} %bitcast.40, () %tuple.216, (f32[2,256]{1,0:T(2,128)S(1)}, ...), branch_computations={%region_43.0_spmd, %region_44.0_spmd} | conditional | flops 1073741824 | bytes 28344496 | solution.py:312
  302.8 5.2 %all-to-all-start.39 = ((bf16[8,32,2048]{2,1,0:T(8,128)(2,1)}), bf16[8,32,2048]{2,1,0:T(8,128)(2,1)}, u32[]{:S(2)}, u32[]{:S(2)}) async-start(bf16[8,32,2048]{2,1,0:T(8,128)(2,1)} %get-tuple-element.752), calls=%async_computation.39 | async-start | bytes 2097152 | tf_op jit(solution)/shard_map/cond/branch_1_fun/all_to_all | solution.py:166
  310.5 8.5 %own.1 = (bf16[256,2048]{1,0:T(8,128)(2,1)}, bf16[256,2048]{1,0:T(8,128)(2,1)}, bf16[256,2048]{1,0:T(8,128)(2,1)}, bf16[256,2048]{1,0:T(8,128)(2,1)}) custom-call(f32[2,256]{1,0:T(2,128)S(1)} %get-tuple-element.736.sums, bf16[16,256,256]{2,1,0:T(8,128)(2,1)} %get-tuple-element.737.po, bf16[256,2048]{1,0:T(8,128)(2,1)} %get-tuple-element.738.dattn, ...), custom_call_target="tpu_custom_call" | custom-call | flops 1073741824 | bytes 11534336 | tf_op jit(solution)/shard_map/cond/branch_1_fun/own/pallas_call | solution.py:465
  319.0 2.9 finish.2
  321.9 5.6 %collective-permute-done.71 = bf16[128,2048]{1,0:T(8,128)(2,1)} collective-permute-done((bf16[128,2048]{1,0:T(8,128)(2,1)S(1)}, bf16[128,2048]{1,0:T(8,128)(2,1)}, u32[]{:S(2)}, u32[]{:S(2)}) %collective-permute-start.71) | collective-permute-done | bytes 524320 | tf_op jit(solution)/shard_map/cond/branch_1_fun/ppermute | solution.py:151
  328.4 4.1 %finish.3 = bf16[256,2048]{1,0:T(8,128)(2,1)} custom-call(bf16[256,2048]{1,0:T(8,128)(2,1)S(1)} %get-tuple-element.837.own, bf16[256,2048]{1,0:T(8,128)(2,1)} %get-tuple-element.838.home, bf16[128,2048]{1,0:T(8,128)(2,1)} %get-tuple-element.839.near_upper, bf16[128,2048]{1,0:T(8,128)(2,1)} %get-tuple-element.840.near_lower), custom_call_target="tpu_custom_call" | custom-call | bytes 6291456 | tf_op jit(solution)/shard_map/finish/pallas_call | solution.py:462
  (60 shorter events, 28.2 us)
Async XLA Ops:
  1.3 30.8 %copy-start = (bf16[256,2048]{1,0:T(8,128)(2,1)S(1)}, bf16[256,2048]{1,0:T(8,128)(2,1)}, u32[]{:S(2)}) copy-start(bf16[256,2048]{1,0:T(8,128)(2,1)} %param.52) | copy-start | bytes 3145732
  1.3 5.3 %copy-start.2 = (bf16[256,2048]{1,0:T(8,128)(2,1)S(1)}, bf16[256,2048]{1,0:T(8,128)(2,1)}, u32[]{:S(2)}) copy-start(bf16[256,2048]{1,0:T(8,128)(2,1)} %get-tuple-element.426) | copy-start | bytes 3145732 | tf_op jit(solution)/shard_map/cond
  1.3 8.4 %copy-start.56 = (s32[16]{0:T(128)S(1)}, s32[16]{0:T(128)}, u32[]{:S(2)}) copy-start(s32[16]{0:T(128)} %get-tuple-element.428.pairing) | copy-start | bytes 196 | tf_op jit(solution)/shard_map/cond
  1.3 29.4 %all-to-all-start = ((bf16[8,32,2048]{2,1,0:T(8,128)(2,1)}), bf16[8,32,2048]{2,1,0:T(8,128)(2,1)}, u32[]{:S(2)}, u32[]{:S(2)}) async-start(bf16[8,32,2048]{2,1,0:T(8,128)(2,1)} %bitcast.55), calls=%async_computation | async-start | bytes 2097152 | tf_op jit(solution)/shard_map/cond/branch_1_fun/all_to_all | solution.py:166
  6.6 24.1 %collective-permute-start = (bf16[128,2048]{1,0:T(8,128)(2,1)S(1)}, bf16[128,2048]{1,0:T(8,128)(2,1)}, u32[]{:S(2)}, u32[]{:S(2)}) collective-permute-start(bf16[128,2048]{1,0:T(8,128)(2,1)S(1)} %slice.77), channel_id=1, source_target_pairs={{0,2},{2,4},{4,6},{6,8},{8,10},{10,12},{12,14},{14,16},{16,18},{18... | collective-permute-start | bytes 1572872 | tf_op jit(solution)/shard_map/cond/branch_1_fun/ppermute | solution.py:151
  32.1 10.5 %copy-start.8 = (bf16[256,2048]{1,0:T(8,128)(2,1)S(1)}, bf16[256,2048]{1,0:T(8,128)(2,1)}, u32[]{:S(2)}) copy-start(bf16[256,2048]{1,0:T(8,128)(2,1)} %get-tuple-element.477) | copy-start | bytes 3145732 | tf_op jit(solution)/shard_map/cond
  34.7 5.3 %copy-start.26 = (bf16[5,32,2048]{2,1,0:T(8,128)(2,1)S(1)}, bf16[5,32,2048]{2,1,0:T(8,128)(2,1)}, u32[]{:S(2)}) copy-start(bf16[5,32,2048]{2,1,0:T(8,128)(2,1)} %pick.77) | copy-start | bytes 1966084 | tf_op jit(solution)/shard_map/cond
  34.7 46.9 %all-to-all-start.6 = ((bf16[8,32,2048]{2,1,0:T(8,128)(2,1)S(1)}), bf16[8,32,2048]{2,1,0:T(8,128)(2,1)}, u32[]{:S(2)}, u32[]{:S(2)}) async-start(bf16[8,32,2048]{2,1,0:T(8,128)(2,1)S(1)} %bitcast.51), calls=%async_computation.6 | async-start | bytes 2097152 | tf_op jit(solution)/shard_map/cond/branch_5_fun/all_to_all | solution.py:166
  40.0 31.9 %collective-permute-start.10 = (bf16[5,32,2048]{2,1,0:T(8,128)(2,1)S(1)}, bf16[5,32,2048]{2,1,0:T(8,128)(2,1)S(1)}, u32[]{:S(2)}, u32[]{:S(2)}) collective-permute-start(bf16[5,32,2048]{2,1,0:T(8,128)(2,1)S(1)} %copy-done.26), channel_id=1, source_target_pairs={{0,16},{2,18},{4,20},{6,22},{8,24},{10,26},{12,28},{14,30},{16,0},... | collective-permute-start | bytes 1966088 | tf_op jit(solution)/shard_map/cond/branch_5_fun/ppermute | solution.py:289
  43.4 38.2 %collective-permute-start.11 = (bf16[128,2048]{1,0:T(8,128)(2,1)}, bf16[128,2048]{1,0:T(8,128)(2,1)}, u32[]{:S(2)}, u32[]{:S(2)}) collective-permute-start(bf16[128,2048]{1,0:T(8,128)(2,1)} %slice.91), channel_id=1, source_target_pairs={{0,2},{2,4},{4,6},{6,8},{8,10},{10,12},{12,14},{14,16},{16,18},{18... | collective-permute-start | bytes 1572872 | tf_op jit(solution)/shard_map/cond/branch_5_fun/ppermute | solution.py:151
  71.9 0.8 copy-start.27
  81.7 50.7 %copy-start.1 = (bf16[256,2048]{1,0:T(8,128)(2,1)S(1)}, bf16[256,2048]{1,0:T(8,128)(2,1)}, u32[]{:S(2)}) copy-start(bf16[256,2048]{1,0:T(8,128)(2,1)} %param.51) | copy-start | bytes 3145732
  81.7 50.7 %copy-start.15 = (bf16[256,2048]{1,0:T(8,128)(2,1)S(1)}, bf16[256,2048]{1,0:T(8,128)(2,1)}, u32[]{:S(2)}) copy-start(bf16[256,2048]{1,0:T(8,128)(2,1)} %param.50) | copy-start | bytes 3145732
  84.3 48.0 %all-to-all-start.15 = ((bf16[8,32,2048]{2,1,0:T(8,128)(2,1)}), bf16[8,32,2048]{2,1,0:T(8,128)(2,1)}, u32[]{:S(2)}, u32[]{:S(2)}) async-start(bf16[8,32,2048]{2,1,0:T(8,128)(2,1)} %get-tuple-element.546), calls=%async_computation.15 | async-start | bytes 2097152 | tf_op jit(solution)/shard_map/cond/branch_5_fun/all_to_all | solution.py:166
  89.4 34.4 %collective-permute-start.27 = (bf16[5,32,2048]{2,1,0:T(8,128)(2,1)}, bf16[5,32,2048]{2,1,0:T(8,128)(2,1)}, u32[]{:S(2)}, u32[]{:S(2)}) collective-permute-start(bf16[5,32,2048]{2,1,0:T(8,128)(2,1)} %pick.94), channel_id=1, source_target_pairs={{0,16},{2,18},{4,20},{6,22},{8,24},{10,26},{12,28},{14,30},{16,0},... | collective-permute-start | bytes 1966088 | tf_op jit(solution)/shard_map/cond/branch_5_fun/ppermute | solution.py:289
  95.1 37.3 %collective-permute-start.28 = (bf16[128,2048]{1,0:T(8,128)(2,1)}, bf16[128,2048]{1,0:T(8,128)(2,1)}, u32[]{:S(2)}, u32[]{:S(2)}) collective-permute-start(bf16[128,2048]{1,0:T(8,128)(2,1)} %slice.100), channel_id=1, source_target_pairs={{0,2},{2,4},{4,6},{6,8},{8,10},{10,12},{12,14},{14,16},{16,18},{18... | collective-permute-start | bytes 1572872 | tf_op jit(solution)/shard_map/cond/branch_5_fun/ppermute | solution.py:151
  132.4 26.4 %copy-start.54 = (f32[2048]{0:T(1024)S(1)}, f32[2048]{0:T(1024)}, u32[]{:S(2)}) copy-start(f32[2048]{0:T(1024)} %param.54) | copy-start | bytes 24580
  132.4 26.4 %all-to-all-start.19 = ((bf16[8,32,2048]{2,1,0:T(8,128)(2,1)}), bf16[8,32,2048]{2,1,0:T(8,128)(2,1)}, u32[]{:S(2)}, u32[]{:S(2)}) async-start(bf16[8,32,2048]{2,1,0:T(8,128)(2,1)} %get-tuple-element.582), calls=%async_computation.19 | async-start | bytes 2097152 | tf_op jit(solution)/shard_map/cond/branch_1_fun/all_to_all | solution.py:166
  137.6 21.2 %collective-permute-start.35 = (bf16[128,2048]{1,0:T(8,128)(2,1)S(1)}, bf16[128,2048]{1,0:T(8,128)(2,1)}, u32[]{:S(2)}, u32[]{:S(2)}) collective-permute-start(bf16[128,2048]{1,0:T(8,128)(2,1)S(1)} %slice.104), channel_id=1, source_target_pairs={{0,2},{2,4},{4,6},{6,8},{8,10},{10,12},{12,14},{14,16},{16,18},{18... | collective-permute-start | bytes 1572872 | tf_op jit(solution)/shard_map/cond/branch_1_fun/ppermute | solution.py:151
  164.5 7.8 %copy-start.12 = (bf16[256,2048]{1,0:T(8,128)(2,1)}, bf16[256,2048]{1,0:T(8,128)(2,1)S(1)}, u32[]{:S(2)}) copy-start(bf16[256,2048]{1,0:T(8,128)(2,1)S(1)} %get-tuple-element.818.attn) | copy-start | bytes 3145732
  172.3 5.4 %copy-start.13 = (bf16[256,2048]{1,0:T(8,128)(2,1)}, bf16[256,2048]{1,0:T(8,128)(2,1)S(1)}, u32[]{:S(2)}) copy-start(bf16[256,2048]{1,0:T(8,128)(2,1)S(1)} %get-tuple-element.586.attn) | copy-start | bytes 3145732 | tf_op jit(solution)/shard_map/cond
  172.3 34.0 %all-to-all-start.20 = ((bf16[8,32,2048]{2,1,0:T(8,128)(2,1)}), bf16[8,32,2048]{2,1,0:T(8,128)(2,1)}, u32[]{:S(2)}, u32[]{:S(2)}) async-start(bf16[8,32,2048]{2,1,0:T(8,128)(2,1)} %bitcast.56), calls=%async_computation.20 | async-start | bytes 2097152 | tf_op jit(solution)/shard_map/cond/branch_1_fun/all_to_all | solution.py:166
  177.7 11.8 %copy-start.14 = (bf16[256,2048]{1,0:T(8,128)(2,1)S(1)}, bf16[256,2048]{1,0:T(8,128)(2,1)}, u32[]{:S(2)}) copy-start(bf16[256,2048]{1,0:T(8,128)(2,1)} %copy-done.13) | copy-start | bytes 3145732 | tf_op jit(solution)/shard_map/cond
  177.7 11.8 %copy-start.16 = (bf16[256,2048]{1,0:T(8,128)(2,1)S(1)}, bf16[256,2048]{1,0:T(8,128)(2,1)}, u32[]{:S(2)}) copy-start(bf16[256,2048]{1,0:T(8,128)(2,1)} %get-tuple-element.587.q) | copy-start | bytes 3145732 | tf_op jit(solution)/shard_map/cond
  177.7 11.8 %copy-start.17 = (bf16[256,2048]{1,0:T(8,128)(2,1)S(1)}, bf16[256,2048]{1,0:T(8,128)(2,1)}, u32[]{:S(2)}) copy-start(bf16[256,2048]{1,0:T(8,128)(2,1)} %get-tuple-element.585.dattn) | copy-start | bytes 3145732 | tf_op jit(solution)/shard_map/cond
  187.0 19.3 %collective-permute-start.36 = (bf16[128,2048]{1,0:T(8,128)(2,1)S(1)}, bf16[128,2048]{1,0:T(8,128)(2,1)}, u32[]{:S(2)}, u32[]{:S(2)}) collective-permute-start(bf16[128,2048]{1,0:T(8,128)(2,1)S(1)} %slice.105), channel_id=1, source_target_pairs={{2,0},{4,2},{6,4},{8,6},{10,8},{12,10},{14,12},{16,14},{18,16},{20... | collective-permute-start | bytes 1572872 | tf_op jit(solution)/shard_map/cond/branch_1_fun/ppermute | solution.py:151
  208.9 46.6 %all-to-all-start.26 = ((bf16[8,32,2048]{2,1,0:T(8,128)(2,1)}), bf16[8,32,2048]{2,1,0:T(8,128)(2,1)}, u32[]{:S(2)}, u32[]{:S(2)}) async-start(bf16[8,32,2048]{2,1,0:T(8,128)(2,1)} %bitcast.26), calls=%async_computation.26 | async-start | bytes 2097152 | tf_op jit(solution)/shard_map/cond/branch_5_fun/all_to_all | solution.py:166
  214.0 30.7 %collective-permute-start.46 = (bf16[5,32,2048]{2,1,0:T(8,128)(2,1)}, bf16[5,32,2048]{2,1,0:T(8,128)(2,1)}, u32[]{:S(2)}, u32[]{:S(2)}) collective-permute-start(bf16[5,32,2048]{2,1,0:T(8,128)(2,1)} %pick.111), channel_id=1, source_target_pairs={{0,16},{2,18},{4,20},{6,22},{8,24},{10,26},{12,28},{14,30},{16,0},... | collective-permute-start | bytes 1966088 | tf_op jit(solution)/shard_map/cond/branch_5_fun/ppermute | solution.py:289
  219.6 35.9 %collective-permute-start.47 = (bf16[128,2048]{1,0:T(8,128)(2,1)}, bf16[128,2048]{1,0:T(8,128)(2,1)}, u32[]{:S(2)}, u32[]{:S(2)}) collective-permute-start(bf16[128,2048]{1,0:T(8,128)(2,1)} %slice.111), channel_id=1, source_target_pairs={{2,0},{4,2},{6,4},{8,6},{10,8},{12,10},{14,12},{16,14},{18,16},{20... | collective-permute-start | bytes 1572872 | tf_op jit(solution)/shard_map/cond/branch_5_fun/ppermute | solution.py:151
  258.1 44.7 %all-to-all-start.35 = ((bf16[8,32,2048]{2,1,0:T(8,128)(2,1)}), bf16[8,32,2048]{2,1,0:T(8,128)(2,1)}, u32[]{:S(2)}, u32[]{:S(2)}) async-start(bf16[8,32,2048]{2,1,0:T(8,128)(2,1)} %get-tuple-element.711), calls=%async_computation.35 | async-start | bytes 2097152 | tf_op jit(solution)/shard_map/cond/branch_5_fun/all_to_all | solution.py:166
  263.2 26.5 %collective-permute-start.63 = (bf16[5,32,2048]{2,1,0:T(8,128)(2,1)}, bf16[5,32,2048]{2,1,0:T(8,128)(2,1)}, u32[]{:S(2)}, u32[]{:S(2)}) collective-permute-start(bf16[5,32,2048]{2,1,0:T(8,128)(2,1)} %pick.128), channel_id=1, source_target_pairs={{0,16},{2,18},{4,20},{6,22},{8,24},{10,26},{12,28},{14,30},{16,0},... | collective-permute-start | bytes 1966088 | tf_op jit(solution)/shard_map/cond/branch_5_fun/ppermute | solution.py:289
  264.1 38.7 %collective-permute-start.64 = (bf16[128,2048]{1,0:T(8,128)(2,1)}, bf16[128,2048]{1,0:T(8,128)(2,1)}, u32[]{:S(2)}, u32[]{:S(2)}) collective-permute-start(bf16[128,2048]{1,0:T(8,128)(2,1)} %slice.120), channel_id=1, source_target_pairs={{2,0},{4,2},{6,4},{8,6},{10,8},{12,10},{14,12},{16,14},{18,16},{20... | collective-permute-start | bytes 1572872 | tf_op jit(solution)/shard_map/cond/branch_5_fun/ppermute | solution.py:151
  302.8 7.8 %copy-start.55 = (f32[1,2048]{1,0:T(1,128)S(1)}, f32[1,2048]{1,0:T(1,128)}, u32[]{:S(2)}) copy-start(f32[1,2048]{1,0:T(1,128)} %get-tuple-element.744.gain) | copy-start | bytes 24580 | tf_op jit(solution)/shard_map/cond
  302.8 25.6 %all-to-all-start.39 = ((bf16[8,32,2048]{2,1,0:T(8,128)(2,1)}), bf16[8,32,2048]{2,1,0:T(8,128)(2,1)}, u32[]{:S(2)}, u32[]{:S(2)}) async-start(bf16[8,32,2048]{2,1,0:T(8,128)(2,1)} %get-tuple-element.752), calls=%async_computation.39 | async-start | bytes 2097152 | tf_op jit(solution)/shard_map/cond/branch_1_fun/all_to_all | solution.py:166
  308.1 19.5 %collective-permute-start.71 = (bf16[128,2048]{1,0:T(8,128)(2,1)S(1)}, bf16[128,2048]{1,0:T(8,128)(2,1)}, u32[]{:S(2)}, u32[]{:S(2)}) collective-permute-start(bf16[128,2048]{1,0:T(8,128)(2,1)S(1)} %slice.124), channel_id=1, source_target_pairs={{2,0},{4,2},{6,4},{8,6},{10,8},{12,10},{14,12},{16,14},{18,16},{20... | collective-permute-start | bytes 1572872 | tf_op jit(solution)/shard_map/cond/branch_1_fun/ppermute | solution.py:151
  319.0 9.3 %copy-start.18 = (bf16[256,2048]{1,0:T(8,128)(2,1)S(1)}, bf16[256,2048]{1,0:T(8,128)(2,1)}, u32[]{:S(2)}) copy-start(bf16[256,2048]{1,0:T(8,128)(2,1)} %get-tuple-element.999) | copy-start | bytes 3145732 | tf_op jit(solution)/shard_map/cond
  328.4 4.1 %copy-start.21 = (bf16[256,2048]{1,0:T(8,128)(2,1)}, bf16[256,2048]{1,0:T(8,128)(2,1)S(1)}, u32[]{:S(2)}) copy-start(bf16[256,2048]{1,0:T(8,128)(2,1)S(1)} %get-tuple-element.799) | copy-start | bytes 3145732
